TPU v7x, 256 devices: a whole 4x4x8 slice. The times are simulated.
256 devices in a mesh: section: 8 (over z_lo, x), expert: 32 (over y, z_hi, core).
Axes of the slice: x: 4, y: 4, z: 8 (z_hi: 4, z_lo: 2; z = z_hi * 2 + z_lo), core: 2. Of those that a mesh axis runs over, the one named last changes fastest.
Arguments:
- forward_batch: bfloat16 [8, 2048, 7168], P('section', 'expert'), may hold values from -6 to 6
- reverse_batch: bfloat16 [8, 2048, 7168], P('section', 'expert'), may hold values from -6 to 6
- norm_gain: float32 [8, 7168], P('section'), may hold values from 0.1 to 1.9
- routes: int32 [8, 2, 2, 2048, 1], P('section', None, None, 'expert'), may hold values from 0 to 7; in each aligned block of 64 rows (0 to 63, 64 to 127, ..., all dimensions but the last counted through in order) at most 8 rows name the same one
- gate_values: float32 [8, 2, 2, 2048, 1], P('section', None, None, 'expert'), may hold values from 0.2 to 1
- up_weight: bfloat16 [8, 32, 7168, 256], P('section', 'expert'), may hold values from -0.0625 to 0.0625
- down_weight: bfloat16 [8, 32, 256, 7168], P('section', 'expert'), may hold values from -0.1875 to 0.1875
Outputs:
- forward_out: bfloat16 [8, 2048, 7168], P('section', 'expert')
- reverse_out: bfloat16 [8, 2048, 7168], P('section', 'expert')
Inputs may be any that keep to these rules, and one draw needn't show every extreme that they name: `routes`: each token names exactly one expert; for each section, direction and step, the 64 tokens of one device name every expert exactly 8 times.
All inputs are finite; a program needn't handle non-finite values.
Results may differ from a plain program's by a relative error of at most 0.006.
Values may be sent and summed in bfloat16 or wider, within the bound.
No kernel may reach another device: no remote copies, remote signals or barrier semaphores. Data moves between devices by JAX's collectives and lax.ppermute only.
A program may use at most 128 MiB of HBM per device.

v0:
```python
import jax
import jax.numpy as jnp
from jax import lax
from jax.sharding import PartitionSpec as P

SPLIT = 4
TOP = 1
STEPS = 2


epsilon = 1e-06


def passed_along(array, axis, by):
    size = lax.axis_size(axis)
    return lax.ppermute(array, axis, [(i, (i + by) % size) for i in range(size)])


def slot_matrix(route_flat, experts, capacity):
    chosen = (route_flat[:, None] == jnp.arange(experts, dtype=jnp.int32)[None, :]).astype(
        jnp.int32
    )
    before = jnp.cumsum(chosen, axis=0) - chosen
    position = jnp.sum(chosen * before, axis=1)
    target = route_flat * capacity + position
    return (target[:, None] == jnp.arange(experts * capacity, dtype=jnp.int32)[None, :]).astype(
        jnp.bfloat16
    )


def run_slice(arrived, up_matrix, down_matrix):
    layout = arrived.shape
    flattened = arrived.reshape(-1, layout[-1])
    up_values = jnp.dot(flattened, up_matrix, preferred_element_type=jnp.float32)
    activated = jax.nn.silu(up_values).astype(jnp.bfloat16)
    partial_value = jnp.dot(activated, down_matrix, preferred_element_type=jnp.float32).astype(
        jnp.bfloat16
    )
    return partial_value.reshape(layout)


def prepare(current, norm_scale, route, experts, capacity, devices):
    width = current.shape[1]
    as_float = current.astype(jnp.float32)
    normed = (
        as_float
        * lax.rsqrt(jnp.mean(as_float * as_float, axis=-1, keepdims=True) + epsilon)
        * norm_scale
    ).astype(jnp.bfloat16)
    slot_table = slot_matrix(route.reshape(-1), experts, capacity)
    token_rows = jnp.repeat(normed, TOP, axis=0)
    sending = jnp.einsum(
        "as,ad->sd", slot_table, token_rows, preferred_element_type=jnp.float32
    ).astype(jnp.bfloat16)
    copies = jnp.broadcast_to(
        sending.reshape(experts, 1, capacity, width), (experts, SPLIT, capacity, width)
    )
    return (copies.reshape(devices, capacity, width), slot_table, sending)


def add_slices(returned, experts, capacity):
    width = returned.shape[-1]
    summed = jnp.sum(returned.reshape(experts, SPLIT, capacity, width).astype(jnp.float32), axis=1)
    return summed.astype(jnp.bfloat16).reshape(experts * capacity, width)


def finish(current, slot_table, produced, weighting):
    width = current.shape[1]
    gathered = jnp.einsum("as,sd->ad", slot_table, produced, preferred_element_type=jnp.float32)
    mixed = jnp.sum(gathered.reshape(current.shape[0], TOP, width) * weighting[:, :, None], axis=1)
    return (current.astype(jnp.float32) + mixed).astype(jnp.bfloat16)


def round_trip(sending, expert_rows):
    results = expert_rows(
        lax.all_to_all(sending, "expert", split_axis=0, concat_axis=0, tiled=True)
    )
    return lax.all_to_all(results, "expert", split_axis=0, concat_axis=0, tiled=True)


def per_device(
    forward_batch, reverse_batch, norm_gain, routes, gate_values, up_weight, down_weight
):
    up_matrix = up_weight[0, 0]
    down_matrix = down_weight[0, 0]
    norm_scale = norm_gain[0]
    devices = lax.axis_size("expert")
    experts = devices // SPLIT
    capacity = forward_batch.shape[1] * TOP * SPLIT // devices
    states = [forward_batch[0], reverse_batch[0]]

    def expert_rows(arrived):
        return run_slice(arrived, up_matrix, down_matrix)

    for moment in range(STEPS):
        prepared = [
            prepare(
                states[course], norm_scale, routes[0, course, moment], experts, capacity, devices
            )
            for course in range(2)
        ]
        outputs = [
            add_slices(round_trip(prepared[course][0], expert_rows), experts, capacity)
            for course in range(2)
        ]
        states = [
            finish(
                states[course], prepared[course][1], outputs[course], gate_values[0, course, moment]
            )
            for course in range(2)
        ]
        if moment + 1 < STEPS:
            states[0] = passed_along(states[0], "section", 1)
            states[1] = passed_along(states[1], "section", -1)
    return (states[0][None], states[1][None])


def solution(mesh):
    return jax.shard_map(
        per_device,
        mesh=mesh,
        in_specs=(
            P("section", "expert", None),
            P("section", "expert", None),
            P("section", None),
            P("section", None, None, "expert", None),
            P("section", None, None, "expert", None),
            P("section", "expert", None, None),
            P("section", "expert", None, None),
        ),
        out_specs=(P("section", "expert", None), P("section", "expert", None)),
        check_vma=False,
    )
```

profile of v0, /device:TPU:7, one launch (start us, length us, event | category | flops | bytes accessed | tf_op | source)
XLA Modules:
  0.0 788.7 jit_solution(6771128866446025945)
XLA Ops:
  0.6 0.7 slice_bitcast_fusion.1
  1.3 0.1 fusion.103
  1.4 0.1 fusion.102
  1.5 0.1 reduce_window_sum.22
  1.6 0.1 reduce_window_sum.23
  1.7 0.1 fusion.101
  1.8 0.1 reduce_window_sum.27
  1.9 0.1 fusion.100
  1.9 0.1 reduce_window_sum.32
  2.0 1.5 fusion.43
  3.5 0.2 select_reduce_fusion.2
  3.7 0.2 select_reduce_fusion
  3.9 0.7 multiply_add_fusion
  4.6 1.7 fusion.14
  6.3 2.2 broadcast_in_dim.26
  8.5 0.0 copy-start.1
  8.5 0.0 copy-start.2
  8.6 12.1 %all-to-all-start.4 = ((bf16[32,8,7168]{2,1,0:T(8,128)(2,1)}), bf16[32,8,7168]{2,1,0:T(8,128)(2,1)}, u32[]{:S(2)}, u32[]{:S(2)}) async-start(bf16[32,8,7168]{2,1,0:T(8,128)(2,1)} %bitcast.148), calls=%async_computation.4 | async-start | bytes 7340032 | tf_op jit(solution)/shard_map/all_to_all | solution.py:76
  20.7 0.0 copy-done.1
  20.7 0.3 fusion.40
  21.0 0.0 copy-done.2
  21.0 0.5 fusion.12
  21.5 84.4 %all-to-all-done.4 = bf16[32,8,7168]{2,1,0:T(8,128)(2,1)} async-done(((bf16[32,8,7168]{2,1,0:T(8,128)(2,1)}), bf16[32,8,7168]{2,1,0:T(8,128)(2,1)}, u32[]{:S(2)}, u32[]{:S(2)}) %all-to-all-start.4) | async-done | bytes 3670048 | tf_op jit(solution)/shard_map/all_to_all | solution.py:76
  105.9 2.4 broadcast_in_dim.21
  108.2 5.9 all-to-all-start
  114.1 10.1 %fusion.2 = bf16[32,8,7168]{2,1,0:T(8,128)(2,1)} fusion(bf16[1,1,256,7168]{3,2,1,0:T(8,128)(2,1)} %param.13, bf16[1,1,7168,256]{3,2,1,0:T(8,128)(2,1)} %param.12, bf16[32,8,7168]{2,1,0:T(8,128)(2,1)} %all-to-all-done.4), kind=kOutput, calls=%fused_computation.6 | convolution fusion | flops 1881210880 | bytes 14680064 | tf_op jit(solution)/shard_map/dot_general | solution.py:36
  124.2 64.2 %all-to-all-done = bf16[32,8,7168]{2,1,0:T(8,128)(2,1)} async-done(((bf16[32,8,7168]{2,1,0:T(8,128)(2,1)}), bf16[32,8,7168]{2,1,0:T(8,128)(2,1)}, u32[]{:S(2)}, u32[]{:S(2)}) %all-to-all-start) | async-done | bytes 3670048 | tf_op jit(solution)/shard_map/all_to_all | solution.py:76
  188.3 12.1 %all-to-all-start.5 = ((bf16[32,8,7168]{2,1,0:T(8,128)(2,1)}), bf16[32,8,7168]{2,1,0:T(8,128)(2,1)}, u32[]{:S(2)}, u32[]{:S(2)}) async-start(bf16[32,8,7168]{2,1,0:T(8,128)(2,1)} %fusion.2), calls=%async_computation.5 | async-start | bytes 7340032 | tf_op jit(solution)/shard_map/all_to_all | solution.py:78
  200.5 10.1 %fusion = bf16[32,8,7168]{2,1,0:T(8,128)(2,1)} fusion(bf16[1,1,256,7168]{3,2,1,0:T(8,128)(2,1)} %param.13, bf16[1,1,7168,256]{3,2,1,0:T(8,128)(2,1)} %param.12, bf16[32,8,7168]{2,1,0:T(8,128)(2,1)} %all-to-all-done), kind=kOutput, calls=%fused_computation.4 | convolution fusion | flops 1881210880 | bytes 14680064 | tf_op jit(solution)/shard_map/dot_general | solution.py:36
  210.6 0.0 copy-start.3
  210.6 61.5 %all-to-all-done.5 = bf16[32,8,7168]{2,1,0:T(8,128)(2,1)} async-done(((bf16[32,8,7168]{2,1,0:T(8,128)(2,1)}), bf16[32,8,7168]{2,1,0:T(8,128)(2,1)}, u32[]{:S(2)}, u32[]{:S(2)}) %all-to-all-start.5) | async-done | bytes 3670048 | tf_op jit(solution)/shard_map/all_to_all | solution.py:78
  272.1 18.6 %all-to-all-start.1 = ((bf16[32,8,7168]{2,1,0:T(8,128)(2,1)}), bf16[32,8,7168]{2,1,0:T(8,128)(2,1)}, u32[]{:S(2)}, u32[]{:S(2)}) async-start(bf16[32,8,7168]{2,1,0:T(8,128)(2,1)} %fusion), calls=%async_computation.1 | async-start | bytes 7340032 | tf_op jit(solution)/shard_map/all_to_all | solution.py:78
  290.7 0.0 copy-done.3
  290.7 0.0 copy-start
  290.8 2.6 bitcast_reduce_fusion.1
  293.4 0.0 copy-done
  293.4 0.5 fusion.9
  293.9 3.2 collective-permute-start.1
  297.1 95.4 %collective-permute-done.1 = bf16[64,7168]{1,0:T(8,128)(2,1)S(1)} collective-permute-done((bf16[64,7168]{1,0:T(8,128)(2,1)S(1)}, bf16[64,7168]{1,0:T(8,128)(2,1)S(1)}, u32[]{:S(2)}, u32[]{:S(2)}) %collective-permute-start.1) | collective-permute-done | bytes 917536 | tf_op jit(solution)/shard_map/ppermute | solution.py:16
  392.5 0.3 fusion.37
  392.8 0.5 fusion.15
  393.3 0.0 all-to-all-done.1
  393.3 2.3 broadcast_in_dim.28
  395.7 7.9 %all-to-all-start.6 = ((bf16[32,8,7168]{2,1,0:T(8,128)(2,1)}), bf16[32,8,7168]{2,1,0:T(8,128)(2,1)}, u32[]{:S(2)}, u32[]{:S(2)}) async-start(bf16[32,8,7168]{2,1,0:T(8,128)(2,1)} %bitcast.147), calls=%async_computation.6 | async-start | bytes 7340032 | tf_op jit(solution)/shard_map/all_to_all | solution.py:76
  403.6 2.6 bitcast_reduce_fusion.3
  406.2 0.5 fusion.11
  406.6 0.1 collective-permute-start
  406.7 95.5 %collective-permute-done = bf16[64,7168]{1,0:T(8,128)(2,1)S(1)} collective-permute-done((bf16[64,7168]{1,0:T(8,128)(2,1)S(1)}, bf16[64,7168]{1,0:T(8,128)(2,1)S(1)}, u32[]{:S(2)}, u32[]{:S(2)}) %collective-permute-start) | collective-permute-done | bytes 917536 | tf_op jit(solution)/shard_map/ppermute | solution.py:16
  502.3 0.3 fusion.34
  502.6 0.5 fusion.13
  503.1 0.0 all-to-all-done.6
  503.1 2.4 broadcast_in_dim.23
  505.5 10.1 %all-to-all-start.2 = ((bf16[32,8,7168]{2,1,0:T(8,128)(2,1)}), bf16[32,8,7168]{2,1,0:T(8,128)(2,1)}, u32[]{:S(2)}, u32[]{:S(2)}) async-start(bf16[32,8,7168]{2,1,0:T(8,128)(2,1)} %bitcast.150), calls=%async_computation.2 | async-start | bytes 7340032 | tf_op jit(solution)/shard_map/all_to_all | solution.py:76
  515.6 10.1 %fusion.3 = bf16[32,8,7168]{2,1,0:T(8,128)(2,1)} fusion(bf16[1,1,256,7168]{3,2,1,0:T(8,128)(2,1)} %param.13, bf16[1,1,7168,256]{3,2,1,0:T(8,128)(2,1)} %param.12, bf16[32,8,7168]{2,1,0:T(8,128)(2,1)} %all-to-all-done.6), kind=kOutput, calls=%fused_computation.7 | convolution fusion | flops 1881210880 | bytes 14680064 | tf_op jit(solution)/shard_map/dot_general | solution.py:36
  525.7 75.2 %all-to-all-done.2 = bf16[32,8,7168]{2,1,0:T(8,128)(2,1)} async-done(((bf16[32,8,7168]{2,1,0:T(8,128)(2,1)}), bf16[32,8,7168]{2,1,0:T(8,128)(2,1)}, u32[]{:S(2)}, u32[]{:S(2)}) %all-to-all-start.2) | async-done | bytes 3670048 | tf_op jit(solution)/shard_map/all_to_all | solution.py:76
  600.9 6.3 all-to-all-start.7
  607.2 10.1 %fusion.1 = bf16[32,8,7168]{2,1,0:T(8,128)(2,1)} fusion(bf16[1,1,256,7168]{3,2,1,0:T(8,128)(2,1)} %param.13, bf16[1,1,7168,256]{3,2,1,0:T(8,128)(2,1)} %param.12, bf16[32,8,7168]{2,1,0:T(8,128)(2,1)} %all-to-all-done.2), kind=kOutput, calls=%fused_computation.5 | convolution fusion | flops 1881210880 | bytes 14680064 | tf_op jit(solution)/shard_map/dot_general | solution.py:36
  617.3 75.6 %all-to-all-done.7 = bf16[32,8,7168]{2,1,0:T(8,128)(2,1)} async-done(((bf16[32,8,7168]{2,1,0:T(8,128)(2,1)}), bf16[32,8,7168]{2,1,0:T(8,128)(2,1)}, u32[]{:S(2)}, u32[]{:S(2)}) %all-to-all-start.7) | async-done | bytes 3670048 | tf_op jit(solution)/shard_map/all_to_all | solution.py:78
  692.9 5.0 all-to-all-start.3
  697.9 2.6 bitcast_reduce_fusion
  700.5 82.9 %all-to-all-done.3 = bf16[32,8,7168]{2,1,0:T(8,128)(2,1)} async-done(((bf16[32,8,7168]{2,1,0:T(8,128)(2,1)}), bf16[32,8,7168]{2,1,0:T(8,128)(2,1)}, u32[]{:S(2)}, u32[]{:S(2)}) %all-to-all-start.3) | async-done | bytes 3670048 | tf_op jit(solution)/shard_map/all_to_all | solution.py:78
  783.4 2.6 bitcast_reduce_fusion.2
  785.9 1.4 fusion.17
  787.3 1.4 fusion.16
  (5 shorter events, 0.0 us)
Async XLA Ops:
  8.5 12.1 %copy-start.1 = (bf16[1,64,7168]{2,1,0:T(8,128)(2,1)S(1)}, bf16[1,64,7168]{2,1,0:T(8,128)(2,1)}, u32[]{:S(2)}) copy-start(bf16[1,64,7168]{2,1,0:T(8,128)(2,1)} %param.7) | copy-start | bytes 2752516
  8.5 12.4 %copy-start.2 = (f32[1,7168]{1,0:T(1,128)S(1)}, f32[1,7168]{1,0:T(1,128)}, u32[]{:S(2)}) copy-start(f32[1,7168]{1,0:T(1,128)} %param.9) | copy-start | bytes 86020
  8.6 97.3 %all-to-all-start.4 = ((bf16[32,8,7168]{2,1,0:T(8,128)(2,1)}), bf16[32,8,7168]{2,1,0:T(8,128)(2,1)}, u32[]{:S(2)}, u32[]{:S(2)}) async-start(bf16[32,8,7168]{2,1,0:T(8,128)(2,1)} %bitcast.148), calls=%async_computation.4 | async-start | bytes 7340032 | tf_op jit(solution)/shard_map/all_to_all | solution.py:76
  108.2 80.1 %all-to-all-start = ((bf16[32,8,7168]{2,1,0:T(8,128)(2,1)}), bf16[32,8,7168]{2,1,0:T(8,128)(2,1)}, u32[]{:S(2)}, u32[]{:S(2)}) async-start(bf16[32,8,7168]{2,1,0:T(8,128)(2,1)} %bitcast.149), calls=%async_computation | async-start | bytes 7340032 | tf_op jit(solution)/shard_map/all_to_all | solution.py:76
  188.3 83.7 %all-to-all-start.5 = ((bf16[32,8,7168]{2,1,0:T(8,128)(2,1)}), bf16[32,8,7168]{2,1,0:T(8,128)(2,1)}, u32[]{:S(2)}, u32[]{:S(2)}) async-start(bf16[32,8,7168]{2,1,0:T(8,128)(2,1)} %fusion.2), calls=%async_computation.5 | async-start | bytes 7340032 | tf_op jit(solution)/shard_map/all_to_all | solution.py:78
  210.6 80.1 %copy-start.3 = (f32[1,2,2,64,1]{3,4,2,1,0:T(1,128)S(1)}, f32[1,2,2,64,1]{3,4,2,1,0:T(1,128)}, u32[]{:S(2)}) copy-start(f32[1,2,2,64,1]{3,4,2,1,0:T(1,128)} %param.11) | copy-start | bytes 3076
  272.1 121.2 %all-to-all-start.1 = ((bf16[32,8,7168]{2,1,0:T(8,128)(2,1)}), bf16[32,8,7168]{2,1,0:T(8,128)(2,1)}, u32[]{:S(2)}, u32[]{:S(2)}) async-start(bf16[32,8,7168]{2,1,0:T(8,128)(2,1)} %fusion), calls=%async_computation.1 | async-start | bytes 7340032 | tf_op jit(solution)/shard_map/all_to_all | solution.py:78
  290.7 2.7 copy-start
  293.9 98.6 %collective-permute-start.1 = (bf16[64,7168]{1,0:T(8,128)(2,1)S(1)}, bf16[64,7168]{1,0:T(8,128)(2,1)S(1)}, u32[]{:S(2)}, u32[]{:S(2)}) collective-permute-start(bf16[64,7168]{1,0:T(8,128)(2,1)S(1)} %fusion.9), channel_id=1, source_target_pairs={{0,224},{32,0},{64,32},{96,64},{128,96},{160,128},{192,160},{224,1... | collective-permute-start | bytes 2752520 | tf_op jit(solution)/shard_map/ppermute | solution.py:16
  395.7 107.4 %all-to-all-start.6 = ((bf16[32,8,7168]{2,1,0:T(8,128)(2,1)}), bf16[32,8,7168]{2,1,0:T(8,128)(2,1)}, u32[]{:S(2)}, u32[]{:S(2)}) async-start(bf16[32,8,7168]{2,1,0:T(8,128)(2,1)} %bitcast.147), calls=%async_computation.6 | async-start | bytes 7340032 | tf_op jit(solution)/shard_map/all_to_all | solution.py:76
  406.6 95.6 %collective-permute-start = (bf16[64,7168]{1,0:T(8,128)(2,1)S(1)}, bf16[64,7168]{1,0:T(8,128)(2,1)S(1)}, u32[]{:S(2)}, u32[]{:S(2)}) collective-permute-start(bf16[64,7168]{1,0:T(8,128)(2,1)S(1)} %fusion.11), channel_id=1, source_target_pairs={{0,32},{32,64},{64,96},{96,128},{128,160},{160,192},{192,224},{224... | collective-permute-start | bytes 2752520 | tf_op jit(solution)/shard_map/ppermute | solution.py:16
  505.5 95.4 %all-to-all-start.2 = ((bf16[32,8,7168]{2,1,0:T(8,128)(2,1)}), bf16[32,8,7168]{2,1,0:T(8,128)(2,1)}, u32[]{:S(2)}, u32[]{:S(2)}) async-start(bf16[32,8,7168]{2,1,0:T(8,128)(2,1)} %bitcast.150), calls=%async_computation.2 | async-start | bytes 7340032 | tf_op jit(solution)/shard_map/all_to_all | solution.py:76
  600.9 92.0 %all-to-all-start.7 = ((bf16[32,8,7168]{2,1,0:T(8,128)(2,1)}), bf16[32,8,7168]{2,1,0:T(8,128)(2,1)}, u32[]{:S(2)}, u32[]{:S(2)}) async-start(bf16[32,8,7168]{2,1,0:T(8,128)(2,1)} %fusion.3), calls=%async_computation.7 | async-start | bytes 7340032 | tf_op jit(solution)/shard_map/all_to_all | solution.py:78
  692.9 90.5 %all-to-all-start.3 = ((bf16[32,8,7168]{2,1,0:T(8,128)(2,1)}), bf16[32,8,7168]{2,1,0:T(8,128)(2,1)}, u32[]{:S(2)}, u32[]{:S(2)}) async-start(bf16[32,8,7168]{2,1,0:T(8,128)(2,1)} %fusion.1), calls=%async_computation.3 | async-start | bytes 7340032 | tf_op jit(solution)/shard_map/all_to_all | solution.py:78
where the time goes:
time: 790 us; the launch traced here: 789 us
  waiting for transfers between devices  635 us (80%)
  starting transfers between devices  81.4 us (10%)
  matrix products  47.4 us (6%)
  other arithmetic  14.4 us (2%)
  local copies, waits for them, and re-layouts  10 us (1%)
    all_to_all x4, waiting for transfers between devices, round_trip(): lax.all_to_all(sending, 'expert', split_axis=0, concat_axis=0, tiled=True)  224 us
    all_to_all x4, waiting for transfers between devices, round_trip(): lax.all_to_all(results, 'expert', split_axis=0, concat_axis=0, tiled=True)  220 us
    ppermute x2, waiting for transfers between devices, passed_along(): lax.ppermute(array, axis, [(i, (i + by) % size) for i in range(size)])  191 us
    all_to_all x4, starting transfers between devices, round_trip(): lax.all_to_all(results, 'expert', split_axis=0, concat_axis=0, tiled=True)  42 us
    dot_general x4, matrix products, run_slice(): jnp.dot(activated, down_matrix, preferred_element_type=jnp.float32)  40.5 us
    all_to_all x4, starting transfers between devices, round_trip(): lax.all_to_all(sending, 'expert', split_axis=0, concat_axis=0, tiled=True)  36 us
  transfers between devices with their start and end apart: 10, of which 8 were waited for; matrix products, arithmetic and copies ran while one was open for 7% of the time, Pallas kernels for 0%

commit v1 on v0

v1 whole, which is shorter than its diff:
```python
import jax
import jax.numpy as jnp
from jax import lax
from jax.sharding import PartitionSpec as P

SPLIT = 4
STEPS = 2
CORES = 2
HALVES = SPLIT // CORES

epsilon = 1e-06


def passed_along(array, axis, by):
    size = lax.axis_size(axis)
    return lax.ppermute(array, axis, [(i, (i + by) % size) for i in range(size)])


def swapped(array):
    size = lax.axis_size("expert")
    return lax.ppermute(array, "expert", [(i, i ^ 1) for i in range(size)])


def slot_matrix(route_flat, experts, capacity):
    chosen = (route_flat[:, None] == jnp.arange(experts, dtype=jnp.int32)[None, :]).astype(
        jnp.int32
    )
    before = jnp.cumsum(chosen, axis=0) - chosen
    position = jnp.sum(chosen * before, axis=1)
    target = route_flat * capacity + position
    return (target[:, None] == jnp.arange(experts * capacity, dtype=jnp.int32)[None, :]).astype(
        jnp.bfloat16
    )


def prepare(current, norm_scale, slot_table, experts, capacity):
    width = current.shape[1]
    as_float = current.astype(jnp.float32)
    normed = (
        as_float
        * lax.rsqrt(jnp.mean(as_float * as_float, axis=-1, keepdims=True) + epsilon)
        * norm_scale
    ).astype(jnp.bfloat16)
    rows = jnp.einsum(
        "as,ad->sd", slot_table, normed, preferred_element_type=jnp.float32
    ).astype(jnp.bfloat16)
    part = width // CORES
    rows = rows.reshape(experts, capacity, CORES, part).transpose(0, 2, 1, 3)
    copies = jnp.broadcast_to(rows[:, None], (experts, HALVES, CORES, capacity, part))
    return copies.reshape(experts * SPLIT, capacity, part)


def exchange(blocks):
    return lax.all_to_all(blocks, "expert", split_axis=0, concat_axis=0, tiled=True)


def expert_rows(arrived, up_matrix, down_matrix):
    layout = arrived.shape
    hidden = up_matrix.shape[1] // CORES
    sums = jnp.dot(arrived.reshape(-1, layout[-1]), up_matrix, preferred_element_type=jnp.float32)
    theirs = swapped(sums)
    total = sums + jnp.concatenate([theirs[:, hidden:], theirs[:, :hidden]], axis=1)
    activated = jax.nn.silu(total).astype(jnp.bfloat16)
    partial = jnp.dot(activated, down_matrix, preferred_element_type=jnp.float32)
    return partial.astype(jnp.bfloat16).reshape(layout)


def finish(current, slot_table, returned, weighting, experts, capacity):
    tokens, width = current.shape
    part = width // CORES
    summed = jnp.sum(
        returned.reshape(experts, HALVES, CORES, capacity, part).astype(jnp.float32), axis=1
    ).astype(jnp.bfloat16)
    produced = summed.transpose(0, 2, 1, 3).reshape(experts * capacity, width)
    gathered = jnp.einsum("as,sd->ad", slot_table, produced, preferred_element_type=jnp.float32)
    return (current.astype(jnp.float32) + gathered * weighting).astype(jnp.bfloat16)


def per_device(
    forward_batch, reverse_batch, norm_gain, routes, gate_values, up_weight, down_weight
):
    devices = lax.axis_size("expert")
    experts = devices // SPLIT
    states = [forward_batch[0], reverse_batch[0]]
    tokens, width = states[0].shape
    capacity = tokens // experts
    norm_scale = norm_gain[0]
    part = width // CORES

    core = lax.axis_index("expert") % CORES
    up_own, down_own = up_weight[0, 0], down_weight[0, 0]
    up_kept = lax.dynamic_slice_in_dim(up_own, core * part, part, 0)
    up_given = lax.dynamic_slice_in_dim(up_own, (1 - core) * part, part, 0)
    down_kept = lax.dynamic_slice_in_dim(down_own, core * part, part, 1)
    down_given = lax.dynamic_slice_in_dim(down_own, (1 - core) * part, part, 1)
    up_matrix = jnp.concatenate([up_kept, swapped(up_given)], axis=1)
    down_matrix = jnp.concatenate([down_kept, swapped(down_given)], axis=0)

    tables = [
        [slot_matrix(routes[0, c, t].reshape(-1), experts, capacity) for c in range(2)]
        for t in range(STEPS)
    ]
    for moment in range(STEPS):
        sending = [
            prepare(states[c], norm_scale, tables[moment][c], experts, capacity) for c in range(2)
        ]
        arrived = [exchange(sending[c]) for c in range(2)]
        results = [expert_rows(arrived[c], up_matrix, down_matrix) for c in range(2)]
        returned = [exchange(results[c]) for c in range(2)]
        states = [
            finish(
                states[c],
                tables[moment][c],
                returned[c],
                gate_values[0, c, moment],
                experts,
                capacity,
            )
            for c in range(2)
        ]
        if moment + 1 < STEPS:
            states[0] = passed_along(states[0], "section", 1)
            states[1] = passed_along(states[1], "section", -1)
    return (states[0][None], states[1][None])


def solution(mesh):
    return jax.shard_map(
        per_device,
        mesh=mesh,
        in_specs=(
            P("section", "expert", None),
            P("section", "expert", None),
            P("section", None),
            P("section", None, None, "expert", None),
            P("section", None, None, "expert", None),
            P("section", "expert", None, None),
            P("section", "expert", None, None),
        ),
        out_specs=(P("section", "expert", None), P("section", "expert", None)),
        check_vma=False,
    )
```

time: 790 us -> 475 us (0.60)
  waiting for transfers between devices: 635 us -> 346 us
  matrix products: 47.4 us -> 31.3 us
  starting transfers between devices: 81.4 us -> 69.7 us
    all_to_all x8, waiting for transfers between devices: 444 us -> 220 us  [exchange(): lax.all_to_all(blocks, 'expert', split_axis=0, concat_axis=0, tiled=True)]
    ppermute x2, waiting for transfers between devices: 191 us -> 117 us  [passed_along(): lax.ppermute(array, axis, [(i, (i + by) % size) for i in range(size)])]
    dot_general x8 -> x12, matrix products: 43.8 us -> 27.7 us  [the longest x4 14.8 us: expert_rows(): jnp.dot(arrived.reshape(-1, layout[-1]), up_matrix, preferred_element_typ...]
    all_to_all x8, starting transfers between devices: 78 us -> 66.8 us  [exchange(): lax.all_to_all(blocks, 'expert', split_axis=0, concat_axis=0, tiled=True)]
    ppermute x0 -> x6, waiting for transfers between devices: none -> 8.89 us  [swapped(): return lax.ppermute(array, 'expert', [(i, i ^ 1) for i in range(size)])]
  transfers between devices with their start and end apart: 10 -> 16, of which waited for: 8 -> 13; matrix products, arithmetic and copies ran while one was open for 7% -> 8% of each run, Pallas kernels for 0% -> 0%
where the time goes in v1:
time: 475 us; the launch traced here: 474 us
  waiting for transfers between devices  346 us (73%)
  starting transfers between devices  69.7 us (15%)
  matrix products  31.3 us (7%)
  local copies, waits for them, and re-layouts  13.5 us (3%)
  other arithmetic  12.9 us (3%)
    all_to_all x8, waiting for transfers between devices, exchange(): lax.all_to_all(blocks, 'expert', split_axis=0, concat_axis=0, tiled=True)  220 us
    ppermute x2, waiting for transfers between devices, passed_along(): lax.ppermute(array, axis, [(i, (i + by) % size) for i in range(size)])  117 us
    all_to_all x8, starting transfers between devices, exchange(): lax.all_to_all(blocks, 'expert', split_axis=0, concat_axis=0, tiled=True)  66.8 us
    dot_general x4, matrix products, expert_rows(): jnp.dot(arrived.reshape(-1, layout[-1]), up_matrix, preferred_element_typ...  14.8 us
    dot_general x4, matrix products, expert_rows(): jnp.dot(activated, down_matrix, preferred_element_type=jnp.float32)  9.57 us
  transfers between devices with their start and end apart: 16, of which 13 were waited for; matrix products, arithmetic and copies ran while one was open for 8% of the time, Pallas kernels for 0%

profile of v1, /device:TPU:7, one launch (start us, length us, event | category | flops | bytes accessed | tf_op | source)
XLA Modules:
  0.0 474.3 jit_solution(9496306848746414414)
XLA Ops:
  0.6 0.7 slice_bitcast_fusion.1
  2.0 1.5 fusion.23
  3.9 0.7 multiply_add_fusion
  4.6 1.7 convolution_convert_fusion.1
  6.3 1.4 broadcast_in_dim.15
  7.7 12.1 %all-to-all-start.4 = ((bf16[32,8,3584]{2,1,0:T(8,128)(2,1)}), bf16[32,8,3584]{2,1,0:T(8,128)(2,1)}, u32[]{:S(2)}, u32[]{:S(2)}) async-start(bf16[32,8,3584]{2,1,0:T(8,128)(2,1)} %bitcast.33), calls=%async_computation.4 | async-start | bytes 3670016 | tf_op jit(solution)/shard_map/all_to_all | solution.py:54
  19.9 0.3 fusion.20
  20.2 0.5 convolution_convert_fusion.3
  20.7 44.5 %all-to-all-done.4 = bf16[32,8,3584]{2,1,0:T(8,128)(2,1)} async-done(((bf16[32,8,3584]{2,1,0:T(8,128)(2,1)}), bf16[32,8,3584]{2,1,0:T(8,128)(2,1)}, u32[]{:S(2)}, u32[]{:S(2)}) %all-to-all-start.4) | async-done | bytes 1835040 | tf_op jit(solution)/shard_map/all_to_all | solution.py:54
  65.2 1.5 broadcast_in_dim.12
  66.7 5.7 %all-to-all-start = ((bf16[32,8,3584]{2,1,0:T(8,128)(2,1)}), bf16[32,8,3584]{2,1,0:T(8,128)(2,1)S(1)}, u32[]{:S(2)}, u32[]{:S(2)}) async-start(bf16[32,8,3584]{2,1,0:T(8,128)(2,1)} %bitcast.6), calls=%async_computation | async-start | bytes 3670016 | tf_op jit(solution)/shard_map/all_to_all | solution.py:54
  72.4 2.4 dynamic-slice_bitcast_fusion.3
  74.8 0.4 collective-permute-start
  75.3 0.2 copy-done.3
  75.5 0.2 dynamic-slice_bitcast_fusion.1
  75.8 0.4 collective-permute-start.2
  76.2 2.5 collective-permute-done
  78.7 3.3 fusion.28
  82.0 0.4 collective-permute-start.5
  82.4 1.6 collective-permute-done.5
  84.1 1.2 copy-done.13
  85.3 2.4 fusion.12
  87.7 25.7 %all-to-all-done = bf16[32,8,3584]{2,1,0:T(8,128)(2,1)S(1)} async-done(((bf16[32,8,3584]{2,1,0:T(8,128)(2,1)}), bf16[32,8,3584]{2,1,0:T(8,128)(2,1)S(1)}, u32[]{:S(2)}, u32[]{:S(2)}) %all-to-all-start) | async-done | bytes 1835040 | tf_op jit(solution)/shard_map/all_to_all | solution.py:54
  113.4 1.3 copy-done.5
  114.7 7.5 %all-to-all-start.5 = ((bf16[32,8,3584]{2,1,0:T(8,128)(2,1)}), bf16[32,8,3584]{2,1,0:T(8,128)(2,1)S(1)}, u32[]{:S(2)}, u32[]{:S(2)}) async-start(bf16[32,8,3584]{2,1,0:T(8,128)(2,1)} %fusion.12), calls=%async_computation.5 | async-start | bytes 3670016 | tf_op jit(solution)/shard_map/all_to_all | solution.py:54
  122.2 3.9 fusion.32
  126.0 0.3 collective-permute-start.1
  126.4 1.7 collective-permute-done.1
  128.1 2.4 fusion.10
  130.5 30.5 %all-to-all-done.5 = bf16[32,8,3584]{2,1,0:T(8,128)(2,1)S(1)} async-done(((bf16[32,8,3584]{2,1,0:T(8,128)(2,1)}), bf16[32,8,3584]{2,1,0:T(8,128)(2,1)S(1)}, u32[]{:S(2)}, u32[]{:S(2)}) %all-to-all-start.5) | async-done | bytes 1835040 | tf_op jit(solution)/shard_map/all_to_all | solution.py:54
  161.0 1.2 copy-done.2
  162.3 12.0 %all-to-all-start.1 = ((bf16[32,8,3584]{2,1,0:T(8,128)(2,1)}), bf16[32,8,3584]{2,1,0:T(8,128)(2,1)}, u32[]{:S(2)}, u32[]{:S(2)}) async-start(bf16[32,8,3584]{2,1,0:T(8,128)(2,1)} %fusion.10), calls=%async_computation.1 | async-start | bytes 3670016 | tf_op jit(solution)/shard_map/all_to_all | solution.py:54
  174.3 2.0 reduce_sum.128
  176.2 0.5 fusion.5
  176.7 0.3 collective-permute-start.6
  177.0 59.7 %collective-permute-done.6 = bf16[64,7168]{1,0:T(8,128)(2,1)S(1)} collective-permute-done((bf16[64,7168]{1,0:T(8,128)(2,1)S(1)}, bf16[64,7168]{1,0:T(8,128)(2,1)S(1)}, u32[]{:S(2)}, u32[]{:S(2)}) %collective-permute-start.6) | collective-permute-done | bytes 917536 | tf_op jit(solution)/shard_map/ppermute | solution.py:16
  236.7 0.3 fusion.17
  237.0 0.5 convolution_convert_fusion
  237.5 1.4 broadcast_in_dim.16
  239.0 8.4 %all-to-all-start.6 = ((bf16[32,8,3584]{2,1,0:T(8,128)(2,1)}), bf16[32,8,3584]{2,1,0:T(8,128)(2,1)}, u32[]{:S(2)}, u32[]{:S(2)}) async-start(bf16[32,8,3584]{2,1,0:T(8,128)(2,1)} %bitcast.110), calls=%async_computation.6 | async-start | bytes 3670016 | tf_op jit(solution)/shard_map/all_to_all | solution.py:54
  247.4 1.9 reduce_sum.122
  249.3 0.5 fusion.7
  249.9 57.1 %collective-permute-done.3 = bf16[64,7168]{1,0:T(8,128)(2,1)S(1)} collective-permute-done((bf16[64,7168]{1,0:T(8,128)(2,1)S(1)}, bf16[64,7168]{1,0:T(8,128)(2,1)S(1)}, u32[]{:S(2)}, u32[]{:S(2)}) %collective-permute-start.3) | collective-permute-done | bytes 917536 | tf_op jit(solution)/shard_map/ppermute | solution.py:16
  307.0 0.3 fusion.14
  307.3 0.5 convolution_convert_fusion.2
  307.8 1.5 broadcast_in_dim.13
  309.3 9.4 %all-to-all-start.2 = ((bf16[32,8,3584]{2,1,0:T(8,128)(2,1)}), bf16[32,8,3584]{2,1,0:T(8,128)(2,1)}, u32[]{:S(2)}, u32[]{:S(2)}) async-start(bf16[32,8,3584]{2,1,0:T(8,128)(2,1)} %bitcast.111), calls=%async_computation.2 | async-start | bytes 3670016 | tf_op jit(solution)/shard_map/all_to_all | solution.py:54
  318.8 3.9 fusion.26
  322.6 0.4 collective-permute-start.7
  323.0 1.6 collective-permute-done.7
  324.7 2.4 fusion.13
  327.1 36.7 %all-to-all-done.2 = bf16[32,8,3584]{2,1,0:T(8,128)(2,1)} async-done(((bf16[32,8,3584]{2,1,0:T(8,128)(2,1)}), bf16[32,8,3584]{2,1,0:T(8,128)(2,1)}, u32[]{:S(2)}, u32[]{:S(2)}) %all-to-all-start.2) | async-done | bytes 1835040 | tf_op jit(solution)/shard_map/all_to_all | solution.py:54
  363.8 7.0 %all-to-all-start.7 = ((bf16[32,8,3584]{2,1,0:T(8,128)(2,1)}), bf16[32,8,3584]{2,1,0:T(8,128)(2,1)}, u32[]{:S(2)}, u32[]{:S(2)}) async-start(bf16[32,8,3584]{2,1,0:T(8,128)(2,1)} %fusion.13), calls=%async_computation.7 | async-start | bytes 3670016 | tf_op jit(solution)/shard_map/all_to_all | solution.py:54
  370.9 3.9 fusion.30
  374.7 0.5 collective-permute-start.4
  375.2 1.5 collective-permute-done.4
  376.8 2.4 fusion.11
  379.2 38.2 %all-to-all-done.7 = bf16[32,8,3584]{2,1,0:T(8,128)(2,1)} async-done(((bf16[32,8,3584]{2,1,0:T(8,128)(2,1)}), bf16[32,8,3584]{2,1,0:T(8,128)(2,1)}, u32[]{:S(2)}, u32[]{:S(2)}) %all-to-all-start.7) | async-done | bytes 1835040 | tf_op jit(solution)/shard_map/all_to_all | solution.py:54
  417.4 4.8 %all-to-all-start.3 = ((bf16[32,8,3584]{2,1,0:T(8,128)(2,1)}), bf16[32,8,3584]{2,1,0:T(8,128)(2,1)}, u32[]{:S(2)}, u32[]{:S(2)}) async-start(bf16[32,8,3584]{2,1,0:T(8,128)(2,1)} %fusion.11), calls=%async_computation.3 | async-start | bytes 3670016 | tf_op jit(solution)/shard_map/all_to_all | solution.py:54
  422.1 1.9 reduce_sum.131
  424.0 44.5 %all-to-all-done.3 = bf16[32,8,3584]{2,1,0:T(8,128)(2,1)} async-done(((bf16[32,8,3584]{2,1,0:T(8,128)(2,1)}), bf16[32,8,3584]{2,1,0:T(8,128)(2,1)}, u32[]{:S(2)}, u32[]{:S(2)}) %all-to-all-start.3) | async-done | bytes 1835040 | tf_op jit(solution)/shard_map/all_to_all | solution.py:54
  468.5 3.0 reduce_sum.125
  471.5 1.4 fusion.9
  472.9 1.4 fusion.8
  (55 shorter events, 1.4 us)
Async XLA Ops:
  7.7 12.1 %copy-start.1 = (bf16[1,64,7168]{2,1,0:T(8,128)(2,1)S(1)}, bf16[1,64,7168]{2,1,0:T(8,128)(2,1)}, u32[]{:S(2)}) copy-start(bf16[1,64,7168]{2,1,0:T(8,128)(2,1)} %param.7) | copy-start | bytes 2752516
  7.7 12.4 %copy-start.11 = (f32[1,7168]{1,0:T(1,128)S(1)}, f32[1,7168]{1,0:T(1,128)}, u32[]{:S(2)}) copy-start(f32[1,7168]{1,0:T(1,128)} %param.9) | copy-start | bytes 86020
  7.7 57.4 %all-to-all-start.4 = ((bf16[32,8,3584]{2,1,0:T(8,128)(2,1)}), bf16[32,8,3584]{2,1,0:T(8,128)(2,1)}, u32[]{:S(2)}, u32[]{:S(2)}) async-start(bf16[32,8,3584]{2,1,0:T(8,128)(2,1)} %bitcast.33), calls=%async_computation.4 | async-start | bytes 3670016 | tf_op jit(solution)/shard_map/all_to_all | solution.py:54
  66.7 46.7 %all-to-all-start = ((bf16[32,8,3584]{2,1,0:T(8,128)(2,1)}), bf16[32,8,3584]{2,1,0:T(8,128)(2,1)S(1)}, u32[]{:S(2)}, u32[]{:S(2)}) async-start(bf16[32,8,3584]{2,1,0:T(8,128)(2,1)} %bitcast.6), calls=%async_computation | async-start | bytes 3670016 | tf_op jit(solution)/shard_map/all_to_all | solution.py:54
  72.4 3.1 copy-start.3
  74.8 3.9 copy-start.10
  74.8 3.9 collective-permute-start
  75.8 8.3 %copy-start.6 = (bf16[256,3584]{1,0:T(8,128)(2,1)}, bf16[256,3584]{1,0:T(8,128)(2,1)S(1)}, u32[]{:S(2)}) copy-start(bf16[256,3584]{1,0:T(8,128)(2,1)S(1)} %get-tuple-element.2) | copy-start | bytes 5505028
  75.8 8.3 %collective-permute-start.2 = (bf16[256,3584]{1,0:T(8,128)(2,1)S(1)}, bf16[256,3584]{1,0:T(8,128)(2,1)S(1)}, u32[]{:S(2)}, u32[]{:S(2)}) collective-permute-start(bf16[256,3584]{1,0:T(8,128)(2,1)S(1)} %get-tuple-element.3), channel_id=1, source_target_pairs={{0,1},{1,0},{2,3},{3,2},{4,5},{5,4},{6,7},{7,6},{8,9},{9,8},{10,11... | collective-permute-start | bytes 5505032 | tf_op jit(solution)/shard_map/ppermute | solution.py:21
  78.7 3.3 copy-start.17
  82.0 2.0 collective-permute-start.5
  84.1 1.3 copy-start.13
  113.4 1.3 copy-start.5
  114.7 46.3 %all-to-all-start.5 = ((bf16[32,8,3584]{2,1,0:T(8,128)(2,1)}), bf16[32,8,3584]{2,1,0:T(8,128)(2,1)S(1)}, u32[]{:S(2)}, u32[]{:S(2)}) async-start(bf16[32,8,3584]{2,1,0:T(8,128)(2,1)} %fusion.12), calls=%async_computation.5 | async-start | bytes 3670016 | tf_op jit(solution)/shard_map/all_to_all | solution.py:54
  122.2 5.9 %copy-start.7 = (bf16[256,3584]{1,0:T(8,128)(2,1)S(1)}, bf16[256,3584]{1,0:T(8,128)(2,1)}, u32[]{:S(2)}) copy-start(bf16[256,3584]{1,0:T(8,128)(2,1)} %copy-done.6) | copy-start | bytes 5505028
  122.2 5.9 %copy-start.14 = (bf16[256,3584]{1,0:T(8,128)(2,1)S(1)}, bf16[256,3584]{1,0:T(8,128)(2,1)}, u32[]{:S(2)}) copy-start(bf16[256,3584]{1,0:T(8,128)(2,1)} %copy-done.13) | copy-start | bytes 5505028
  126.0 2.0 collective-permute-start.1
  130.5 43.7 %copy-start.12 = (f32[1,2,2,64,1]{3,4,2,1,0:T(1,128)S(1)}, f32[1,2,2,64,1]{3,4,2,1,0:T(1,128)}, u32[]{:S(2)}) copy-start(f32[1,2,2,64,1]{3,4,2,1,0:T(1,128)} %param.11) | copy-start | bytes 3076
  161.0 1.2 copy-start.2
  162.3 75.2 %all-to-all-start.1 = ((bf16[32,8,3584]{2,1,0:T(8,128)(2,1)}), bf16[32,8,3584]{2,1,0:T(8,128)(2,1)}, u32[]{:S(2)}, u32[]{:S(2)}) async-start(bf16[32,8,3584]{2,1,0:T(8,128)(2,1)} %fusion.10), calls=%async_computation.1 | async-start | bytes 3670016 | tf_op jit(solution)/shard_map/all_to_all | solution.py:54
  174.2 2.0 copy-start
  176.7 60.0 %collective-permute-start.6 = (bf16[64,7168]{1,0:T(8,128)(2,1)S(1)}, bf16[64,7168]{1,0:T(8,128)(2,1)S(1)}, u32[]{:S(2)}, u32[]{:S(2)}) collective-permute-start(bf16[64,7168]{1,0:T(8,128)(2,1)S(1)} %fusion.5), channel_id=1, source_target_pairs={{0,224},{32,0},{64,32},{96,64},{128,96},{160,128},{192,160},{224,1... | collective-permute-start | bytes 2752520 | tf_op jit(solution)/shard_map/ppermute | solution.py:16
  239.0 68.8 %all-to-all-start.6 = ((bf16[32,8,3584]{2,1,0:T(8,128)(2,1)}), bf16[32,8,3584]{2,1,0:T(8,128)(2,1)}, u32[]{:S(2)}, u32[]{:S(2)}) async-start(bf16[32,8,3584]{2,1,0:T(8,128)(2,1)} %bitcast.110), calls=%async_computation.6 | async-start | bytes 3670016 | tf_op jit(solution)/shard_map/all_to_all | solution.py:54
  249.8 57.2 %collective-permute-start.3 = (bf16[64,7168]{1,0:T(8,128)(2,1)S(1)}, bf16[64,7168]{1,0:T(8,128)(2,1)S(1)}, u32[]{:S(2)}, u32[]{:S(2)}) collective-permute-start(bf16[64,7168]{1,0:T(8,128)(2,1)S(1)} %fusion.7), channel_id=1, source_target_pairs={{0,32},{32,64},{64,96},{96,128},{128,160},{160,192},{192,224},{224... | collective-permute-start | bytes 2752520 | tf_op jit(solution)/shard_map/ppermute | solution.py:16
  309.3 54.5 %all-to-all-start.2 = ((bf16[32,8,3584]{2,1,0:T(8,128)(2,1)}), bf16[32,8,3584]{2,1,0:T(8,128)(2,1)}, u32[]{:S(2)}, u32[]{:S(2)}) async-start(bf16[32,8,3584]{2,1,0:T(8,128)(2,1)} %bitcast.111), calls=%async_computation.2 | async-start | bytes 3670016 | tf_op jit(solution)/shard_map/all_to_all | solution.py:54
  318.8 5.9 %copy-start.8 = (bf16[256,3584]{1,0:T(8,128)(2,1)S(1)}, bf16[256,3584]{1,0:T(8,128)(2,1)}, u32[]{:S(2)}) copy-start(bf16[256,3584]{1,0:T(8,128)(2,1)} %copy-done.6) | copy-start | bytes 5505028
  318.8 5.9 %copy-start.15 = (bf16[256,3584]{1,0:T(8,128)(2,1)S(1)}, bf16[256,3584]{1,0:T(8,128)(2,1)}, u32[]{:S(2)}) copy-start(bf16[256,3584]{1,0:T(8,128)(2,1)} %copy-done.13) | copy-start | bytes 5505028
  322.6 2.0 collective-permute-start.7
  363.8 53.5 %all-to-all-start.7 = ((bf16[32,8,3584]{2,1,0:T(8,128)(2,1)}), bf16[32,8,3584]{2,1,0:T(8,128)(2,1)}, u32[]{:S(2)}, u32[]{:S(2)}) async-start(bf16[32,8,3584]{2,1,0:T(8,128)(2,1)} %fusion.13), calls=%async_computation.7 | async-start | bytes 3670016 | tf_op jit(solution)/shard_map/all_to_all | solution.py:54
  370.8 6.0 %copy-start.9 = (bf16[256,3584]{1,0:T(8,128)(2,1)S(1)}, bf16[256,3584]{1,0:T(8,128)(2,1)}, u32[]{:S(2)}) copy-start(bf16[256,3584]{1,0:T(8,128)(2,1)} %copy-done.6) | copy-start | bytes 5505028
  370.8 6.0 %copy-start.16 = (bf16[256,3584]{1,0:T(8,128)(2,1)S(1)}, bf16[256,3584]{1,0:T(8,128)(2,1)}, u32[]{:S(2)}) copy-start(bf16[256,3584]{1,0:T(8,128)(2,1)} %copy-done.13) | copy-start | bytes 5505028
  374.7 2.0 collective-permute-start.4
  417.4 51.2 %all-to-all-start.3 = ((bf16[32,8,3584]{2,1,0:T(8,128)(2,1)}), bf16[32,8,3584]{2,1,0:T(8,128)(2,1)}, u32[]{:S(2)}, u32[]{:S(2)}) async-start(bf16[32,8,3584]{2,1,0:T(8,128)(2,1)} %fusion.11), calls=%async_computation.3 | async-start | bytes 3670016 | tf_op jit(solution)/shard_map/all_to_all | solution.py:54
  471.5 1.4 copy-start.4

commit v2 on v1

v2 whole, which is shorter than its diff:
```python
import functools

import jax
import jax.numpy as jnp
from jax import lax
from jax.experimental import pallas as pl
from jax.experimental.pallas import tpu as pltpu
from jax.sharding import PartitionSpec as P

SPLIT = 4
STEPS = 2
CORES = 2
HALVES = SPLIT // CORES
COURSES = 2
TILE = 512
VMEM_BYTES = 20 * 1024 * 1024

epsilon = 1e-06

F32 = jnp.float32
BF16 = jnp.bfloat16


def passed_along(array, axis, by):
    size = lax.axis_size(axis)
    return lax.ppermute(array, axis, [(i, (i + by) % size) for i in range(size)])


def across_cores(array):
    size = lax.axis_size("expert")
    return lax.ppermute(array, "expert", [(i, i ^ 1) for i in range(size)])


def exchange(blocks):
    return lax.all_to_all(blocks, "expert", split_axis=0, concat_axis=0, tiled=True)


def kernel_call(body, shape, dtype, *operands):
    return pl.pallas_call(
        body,
        out_shape=jax.ShapeDtypeStruct(shape, dtype),
        in_specs=[pl.BlockSpec(memory_space=pltpu.VMEM)] * len(operands),
        out_specs=pl.BlockSpec(memory_space=pltpu.VMEM),
        compiler_params=pltpu.CompilerParams(vmem_limit_bytes=VMEM_BYTES),
    )(*operands)


def tiles(width):
    step = TILE if width % TILE == 0 else width
    return [(start, start + step) for start in range(0, width, step)]


def iota(shape, axis):
    return lax.broadcasted_iota(jnp.int32, shape, axis)


def slots_by_tokens(route, experts, capacity):
    tokens = route.shape[1]
    chosen = (iota((experts, tokens), 0) == route).astype(F32)
    earlier = (iota((tokens, tokens), 0) < iota((tokens, tokens), 1)).astype(BF16)
    before = jnp.dot(chosen.astype(BF16), earlier, preferred_element_type=F32)
    position = jnp.sum(chosen * before, axis=0, keepdims=True).astype(jnp.int32)
    return (iota((experts * capacity, tokens), 0) == route * capacity + position).astype(BF16)


def tokens_by_slots(route, experts, capacity):
    tokens = route.shape[0]
    chosen = (iota((tokens, experts), 1) == route).astype(F32)
    earlier = (iota((tokens, tokens), 1) < iota((tokens, tokens), 0)).astype(BF16)
    before = jnp.dot(earlier, chosen.astype(BF16), preferred_element_type=F32)
    position = jnp.sum(chosen * before, axis=1, keepdims=True).astype(jnp.int32)
    return (iota((tokens, experts * capacity), 1) == route * capacity + position).astype(BF16)


def prepare_body(experts, capacity, first, second, gain, routes, out):
    width = first.shape[1]
    part = width // CORES
    states = (first, second)
    scales, tables = [], []
    for course, state in enumerate(states):
        total = jnp.zeros((state.shape[0], 1), F32)
        for low, high in tiles(width):
            piece = state[:, low:high].astype(F32)
            total = total + jnp.sum(piece * piece, axis=1, keepdims=True)
        scales.append(lax.rsqrt(total / width + epsilon))
        tables.append(slots_by_tokens(routes[course : course + 1, :], experts, capacity))
    for core in range(CORES):
        for low, high in tiles(part):
            columns = slice(core * part + low, core * part + high)
            rows = []
            for state, scale, table in zip(states, scales, tables):
                normed = (state[:, columns].astype(F32) * scale * gain[:, columns]).astype(BF16)
                rows.append(jnp.dot(table, normed, preferred_element_type=F32))
            for e in range(experts):
                span = slice(e * capacity, (e + 1) * capacity)
                block = jnp.concatenate([r[span] for r in rows], axis=0).astype(BF16)
                for half in range(HALVES):
                    out[e * SPLIT + half * CORES + core, :, low:high] = block


def up_body(rows, kept, got, out):
    hidden = kept.shape[1]
    out[:, :hidden] = jnp.dot(rows[...], kept[...], preferred_element_type=F32)
    out[:, hidden:] = jnp.dot(rows[...], got[...], preferred_element_type=F32)


def down_body(mine, theirs, kept, got, out):
    hidden = kept.shape[0]
    first = jax.nn.silu(mine[:, :hidden] + theirs[:, hidden:]).astype(BF16)
    second = jax.nn.silu(mine[:, hidden:] + theirs[:, :hidden]).astype(BF16)
    for low, high in tiles(kept.shape[1]):
        total = jnp.dot(first, kept[:, low:high], preferred_element_type=F32)
        total = total + jnp.dot(second, got[:, low:high], preferred_element_type=F32)
        out[:, low:high] = total.astype(out.dtype)


def finish_body(experts, capacity, course, state, returned, route, gate, out):
    width = state.shape[1]
    part = width // CORES
    table = tokens_by_slots(route[...], experts, capacity)
    span = slice(course * capacity, (course + 1) * capacity)
    for core in range(CORES):
        for low, high in tiles(part):
            columns = slice(core * part + low, core * part + high)
            produced = []
            for e in range(experts):
                blocks = [
                    returned[e * SPLIT + half * CORES + core, :, low:high].astype(F32)[span]
                    for half in range(HALVES)
                ]
                produced.append(sum(blocks))
            produced = jnp.concatenate(produced, axis=0).astype(BF16)
            gathered = jnp.dot(table, produced, preferred_element_type=F32)
            out[:, columns] = (state[:, columns].astype(F32) + gathered * gate[...]).astype(BF16)


def per_device(
    forward_batch, reverse_batch, norm_gain, routes, gate_values, up_weight, down_weight
):
    devices = lax.axis_size("expert")
    experts = devices // SPLIT
    states = [forward_batch[0], reverse_batch[0]]
    tokens, width = states[0].shape
    capacity = tokens // experts
    part = width // CORES
    hidden = up_weight.shape[-1]
    block = (devices, COURSES * capacity, part)

    core = lax.axis_index("expert") % CORES
    up_own, down_own = up_weight[0, 0], down_weight[0, 0]
    up_got = across_cores(lax.dynamic_slice_in_dim(up_own, (1 - core) * part, part, 0))
    down_got = across_cores(lax.dynamic_slice_in_dim(down_own, (1 - core) * part, part, 1))
    up_kept = lax.dynamic_slice_in_dim(up_own, core * part, part, 0)
    down_kept = lax.dynamic_slice_in_dim(down_own, core * part, part, 1)

    for t in range(STEPS):
        sending = kernel_call(
            functools.partial(prepare_body, experts, capacity),
            block,
            BF16,
            *states,
            norm_gain,
            routes[0, :, t, :, 0],
        )
        rows = exchange(sending).reshape(-1, part)
        sums = kernel_call(up_body, (rows.shape[0], hidden * CORES), F32, rows, up_kept, up_got)
        partial = kernel_call(
            down_body, rows.shape, BF16, sums, across_cores(sums), down_kept, down_got
        )
        returned = exchange(partial.reshape(block))
        for c in range(COURSES):
            states[c] = kernel_call(
                functools.partial(finish_body, experts, capacity, c),
                (tokens, width),
                BF16,
                states[c],
                returned,
                routes[0, c, t],
                gate_values[0, c, t],
            )
            if t + 1 < STEPS:
                states[c] = passed_along(states[c], "section", 1 - 2 * c)
    return (states[0][None], states[1][None])


def solution(mesh):
    return jax.shard_map(
        per_device,
        mesh=mesh,
        in_specs=(
            P("section", "expert", None),
            P("section", "expert", None),
            P("section", None),
            P("section", None, None, "expert", None),
            P("section", None, None, "expert", None),
            P("section", "expert", None, None),
            P("section", "expert", None, None),
        ),
        out_specs=(P("section", "expert", None), P("section", "expert", None)),
        check_vma=False,
    )
```

time: 475 us -> 444 us (0.935)
  blocking collectives: 0 us -> 91.8 us
  waiting for transfers between devices: 346 us -> 258 us
  matrix products: 31.3 us -> 0 us
  Pallas kernels: 0 us -> 28.8 us
  starting transfers between devices: 69.7 us -> 43.1 us
  other arithmetic: 12.9 us -> 0 us
  local copies, waits for them, and re-layouts: 13.5 us -> 20.5 us
    ppermute x2, waiting for transfers between devices: 117 us -> 23.3 us  [passed_along(): lax.ppermute(array, axis, [(i, (i + by) % size) for i in range(size)])]
    all_to_all x0 -> x1, blocking collectives: none -> 91.8 us  [exchange(): lax.all_to_all(blocks, 'expert', split_axis=0, concat_axis=0, tiled=True)]
    all_to_all x8 -> x3, starting transfers between devices: 66.8 us -> 21.8 us  [exchange(): lax.all_to_all(blocks, 'expert', split_axis=0, concat_axis=0, tiled=True)]
    dot_general x16 -> x0, matrix products: 31.3 us -> none  [the longest x4 14.8 us: expert_rows(): jnp.dot(arrived.reshape(-1, layout[-1]), up_matrix, preferred_element_typ...]
    pallas_call x0 -> x10, Pallas kernels: none -> 28.8 us  [kernel_call(): pl.pallas_call(body, out_shape=jax.ShapeDtypeStruct(shape, dtype), in_spe...]
    ppermute x2, starting transfers between devices: 0.35 us -> 16.6 us  [passed_along(): lax.ppermute(array, axis, [(i, (i + by) % size) for i in range(size)])]
    reduce_sum x10 -> x0, other arithmetic: 11.4 us -> none  [the longest x4 8.76 us: finish(): jnp.sum(returned.reshape(experts, HALVES, CORES, capacity, part).astype(j...]
    unnamed x36 -> x38, local copies, waits for them, and re-layouts: 4.1 us -> 13.8 us
  transfers between devices with their start and end apart: 16 -> 9, of which waited for: 13 -> 8; matrix products, arithmetic and copies ran while one was open for 8% -> 1% of each run, Pallas kernels for 0% -> 2%
where the time goes in v2:
time: 444 us; the launch traced here: 443 us
  waiting for transfers between devices  258 us (58%)
  blocking collectives  91.8 us (21%)
  starting transfers between devices  43.1 us (10%)
  Pallas kernels  28.8 us (6%)
  local copies, waits for them, and re-layouts  20.5 us (5%)
    all_to_all x3, waiting for transfers between devices, exchange(): lax.all_to_all(blocks, 'expert', split_axis=0, concat_axis=0, tiled=True)  229 us
    all_to_all x1, blocking collectives, exchange(): lax.all_to_all(blocks, 'expert', split_axis=0, concat_axis=0, tiled=True)  91.8 us
    pallas_call x10, Pallas kernels, kernel_call(): pl.pallas_call(body, out_shape=jax.ShapeDtypeStruct(shape, dtype), in_spe...  28.8 us
    ppermute x2, waiting for transfers between devices, passed_along(): lax.ppermute(array, axis, [(i, (i + by) % size) for i in range(size)])  23.3 us
    all_to_all x3, starting transfers between devices, exchange(): lax.all_to_all(blocks, 'expert', split_axis=0, concat_axis=0, tiled=True)  21.8 us
    ppermute x2, starting transfers between devices, passed_along(): lax.ppermute(array, axis, [(i, (i + by) % size) for i in range(size)])  16.6 us
    unnamed x38, local copies, waits for them, and re-layouts  13.8 us
  transfers between devices with their start and end apart: 9, of which 8 were waited for; matrix products, arithmetic and copies ran while one was open for 1% of the time, Pallas kernels for 2%

profile of v2, /device:TPU:7, one launch (start us, length us, event | category | flops | bytes accessed | tf_op | source)
XLA Modules:
  0.0 443.5 jit_solution(13179202714393190911)
XLA Ops:
  0.6 0.7 fusion
  1.3 1.2 copy-done.8
  2.5 1.2 copy-done.10
  3.7 0.7 copy-done.14
  4.4 1.1 shard_map.86
  5.5 0.0 copy-start.4
  5.5 1.8 copy-done.4
  7.4 12.0 %all-to-all-start = ((bf16[32,16,3584]{2,1,0:T(8,128)(2,1)}), bf16[32,16,3584]{2,1,0:T(8,128)(2,1)}, u32[]{:S(2)}, u32[]{:S(2)}) async-start(bf16[32,16,3584]{2,1,0:T(8,128)(2,1)} %copy-done.4), calls=%async_computation | async-start | bytes 7340032 | tf_op jit(solution)/shard_map/all_to_all | solution.py:35
  19.4 0.0 copy-start.16
  19.4 3.8 dynamic-slice_bitcast_fusion.2
  23.1 0.3 collective-permute-start
  23.4 0.0 copy-done.16
  23.4 1.5 dynamic-slice_bitcast_fusion
  24.9 0.2 collective-permute-start.2
  25.1 1.8 collective-permute-done.got
  26.9 1.3 copy-done.5
  28.2 73.3 %all-to-all-done = bf16[32,16,3584]{2,1,0:T(8,128)(2,1)} async-done(((bf16[32,16,3584]{2,1,0:T(8,128)(2,1)}), bf16[32,16,3584]{2,1,0:T(8,128)(2,1)}, u32[]{:S(2)}, u32[]{:S(2)}) %all-to-all-start) | async-done | bytes 3670048 | tf_op jit(solution)/shard_map/all_to_all | solution.py:35
  101.6 1.5 copy-done
  103.1 1.5 copy-done.6
  104.6 4.1 shard_map.87.mine
  108.7 3.2 collective-permute-start.1
  111.9 0.0 collective-permute-done.2.got
  111.9 2.3 collective-permute-done.1.theirs
  114.2 3.6 shard_map.88
  117.8 0.0 copy-start.2
  117.8 1.8 copy-done.2
  119.6 4.9 %all-to-all-start.1 = ((bf16[32,16,3584]{2,1,0:T(8,128)(2,1)}), bf16[32,16,3584]{2,1,0:T(8,128)(2,1)}, u32[]{:S(2)}, u32[]{:S(2)}) async-start(bf16[32,16,3584]{2,1,0:T(8,128)(2,1)} %bitcast.34), calls=%async_computation.1 | async-start | bytes 7340032 | tf_op jit(solution)/shard_map/all_to_all | solution.py:35
  124.5 0.0 copy-done.18
  124.5 0.1 copy.10.gate
  124.6 0.0 copy-done.17
  124.6 0.1 copy.9.route
  124.7 0.1 copy.11.route
  124.8 0.1 copy.12.gate
  124.9 70.5 %all-to-all-done.1.returned = bf16[32,16,3584]{2,1,0:T(8,128)(2,1)} async-done(((bf16[32,16,3584]{2,1,0:T(8,128)(2,1)}), bf16[32,16,3584]{2,1,0:T(8,128)(2,1)}, u32[]{:S(2)}, u32[]{:S(2)}) %all-to-all-start.1) | async-done | bytes 3670048 | tf_op jit(solution)/shard_map/all_to_all | solution.py:35
  195.4 0.0 copy-done.9
  195.4 2.9 shard_map.89
  198.4 0.0 copy-start.15
  198.4 16.5 %collective-permute-start.3 = (bf16[64,7168]{1,0:T(8,128)(2,1)S(1)}, bf16[64,7168]{1,0:T(8,128)(2,1)S(1)}, u32[]{:S(2)}, u32[]{:S(2)}) collective-permute-start(bf16[64,7168]{1,0:T(8,128)(2,1)S(1)} %shard_map.89), channel_id=1, source_target_pairs={{0,32},{32,64},{64,96},{96,128},{128,160},{160,192},{192,224},{224... | collective-permute-start | bytes 2752520 | tf_op jit(solution)/shard_map/ppermute | solution.py:26
  214.9 0.0 copy-done.11
  214.9 2.8 shard_map.90
  217.7 0.1 collective-permute-start.4
  217.8 16.4 %collective-permute-done.3.first.state = bf16[64,7168]{1,0:T(8,128)(2,1)S(1)} collective-permute-done((bf16[64,7168]{1,0:T(8,128)(2,1)S(1)}, bf16[64,7168]{1,0:T(8,128)(2,1)S(1)}, u32[]{:S(2)}, u32[]{:S(2)}) %collective-permute-start.3) | collective-permute-done | bytes 917536 | tf_op jit(solution)/shard_map/ppermute | solution.py:26
  234.2 6.9 %collective-permute-done.4.second.state = bf16[64,7168]{1,0:T(8,128)(2,1)S(1)} collective-permute-done((bf16[64,7168]{1,0:T(8,128)(2,1)S(1)}, bf16[64,7168]{1,0:T(8,128)(2,1)S(1)}, u32[]{:S(2)}, u32[]{:S(2)}) %collective-permute-start.4) | collective-permute-done | bytes 917536 | tf_op jit(solution)/shard_map/ppermute | solution.py:26
  241.1 0.0 copy-done.15
  241.1 1.1 shard_map.91
  242.3 0.0 copy-start.12
  242.3 0.9 copy-done.12
  243.2 91.8 %all_to_all.20 = bf16[32,16,3584]{2,1,0:T(8,128)(2,1)S(1)} all-to-all(bf16[32,16,3584]{2,1,0:T(8,128)(2,1)S(1)} %shard_map.91), channel_id=1, replica_groups=mesh['section'=8,'expert'=32] {'expert'}, dimensions={0} | all-to-all | bytes 7340032 | tf_op jit(solution)/shard_map/all_to_all | solution.py:35
  335.0 0.0 copy-done.1
  335.0 0.0 copy-done.7
  335.0 2.1 shard_map.92.mine
  337.1 1.0 collective-permute-start.5
  338.1 2.3 collective-permute-done.5.theirs
  340.3 3.6 shard_map.93
  343.9 0.0 copy-start.3
  343.9 1.8 copy-done.3
  345.8 4.9 %all-to-all-start.3 = ((bf16[32,16,3584]{2,1,0:T(8,128)(2,1)}), bf16[32,16,3584]{2,1,0:T(8,128)(2,1)}, u32[]{:S(2)}, u32[]{:S(2)}) async-start(bf16[32,16,3584]{2,1,0:T(8,128)(2,1)} %bitcast.35), calls=%async_computation.3 | async-start | bytes 7340032 | tf_op jit(solution)/shard_map/all_to_all | solution.py:35
  350.7 0.1 copy.15.route
  350.8 0.1 copy.16.gate
  350.9 0.1 copy.13.route
  351.0 0.1 copy.14.gate
  351.1 84.9 %all-to-all-done.3.returned = bf16[32,16,3584]{2,1,0:T(8,128)(2,1)} async-done(((bf16[32,16,3584]{2,1,0:T(8,128)(2,1)}), bf16[32,16,3584]{2,1,0:T(8,128)(2,1)}, u32[]{:S(2)}, u32[]{:S(2)}) %all-to-all-start.3) | async-done | bytes 3670048 | tf_op jit(solution)/shard_map/all_to_all | solution.py:35
  436.0 3.7 shard_map.95
  439.7 3.8 shard_map.94
  (16 shorter events, 0.0 us)
Async XLA Ops:
  1.3 1.2 copy-start.8
  2.5 1.2 copy-start.10
  3.7 0.7 copy-start.14
  5.5 1.8 copy-start.4
  7.4 94.2 %all-to-all-start = ((bf16[32,16,3584]{2,1,0:T(8,128)(2,1)}), bf16[32,16,3584]{2,1,0:T(8,128)(2,1)}, u32[]{:S(2)}, u32[]{:S(2)}) async-start(bf16[32,16,3584]{2,1,0:T(8,128)(2,1)} %copy-done.4), calls=%async_computation | async-start | bytes 7340032 | tf_op jit(solution)/shard_map/all_to_all | solution.py:35
  19.4 4.1 copy-start.16
  23.1 3.8 collective-permute-start
  24.9 87.0 %collective-permute-start.2 = (bf16[256,3584]{1,0:T(8,128)(2,1)}, bf16[256,3584]{1,0:T(8,128)(2,1)}, u32[]{:S(2)}, u32[]{:S(2)}) collective-permute-start(bf16[256,3584]{1,0:T(8,128)(2,1)} %get-tuple-element.2), channel_id=1, source_target_pairs={{0,1},{1,0},{2,3},{3,2},{4,5},{5,4},{6,7},{7,6},{8,9},{9,8},{10,11... | collective-permute-start | bytes 5505032 | tf_op jit(solution)/shard_map/ppermute | solution.py:31
  26.9 1.3 copy-start.5
  101.6 1.5 copy-start
  103.1 1.5 copy-start.6
  108.7 5.5 %collective-permute-start.1 = (f32[512,512]{1,0:T(8,128)S(1)}, f32[512,512]{1,0:T(8,128)S(1)}, u32[]{:S(2)}, u32[]{:S(2)}) collective-permute-start(f32[512,512]{1,0:T(8,128)S(1)} %shard_map.87.mine), channel_id=1, source_target_pairs={{0,1},{1,0},{2,3},{3,2},{4,5},{5,4},{6,7},{7,6},{8,9},{9,8},{10,11... | collective-permute-start | bytes 3145736 | tf_op jit(solution)/shard_map/ppermute | solution.py:31
  117.8 1.8 copy-start.2
  119.6 4.9 %copy-start.18 = (f32[1,2,2,64,1]{3,4,2,1,0:T(1,128)S(1)}, f32[1,2,2,64,1]{3,4,2,1,0:T(1,128)}, u32[]{:S(2)}) copy-start(f32[1,2,2,64,1]{3,4,2,1,0:T(1,128)} %param.11) | copy-start | bytes 3076
  119.6 5.0 %copy-start.17 = (s32[1,2,2,64,1]{3,4,2,1,0:T(1,128)S(1)}, s32[1,2,2,64,1]{3,4,2,1,0:T(1,128)}, u32[]{:S(2)}) copy-start(s32[1,2,2,64,1]{3,4,2,1,0:T(1,128)} %param.10) | copy-start | bytes 3076
  119.6 75.8 %copy-start.9 = (bf16[1,64,7168]{2,1,0:T(8,128)(2,1)S(1)}, bf16[1,64,7168]{2,1,0:T(8,128)(2,1)}, u32[]{:S(2)}) copy-start(bf16[1,64,7168]{2,1,0:T(8,128)(2,1)} %param.7) | copy-start | bytes 2752516
  119.6 75.8 %all-to-all-start.1 = ((bf16[32,16,3584]{2,1,0:T(8,128)(2,1)}), bf16[32,16,3584]{2,1,0:T(8,128)(2,1)}, u32[]{:S(2)}, u32[]{:S(2)}) async-start(bf16[32,16,3584]{2,1,0:T(8,128)(2,1)} %bitcast.34), calls=%async_computation.1 | async-start | bytes 7340032 | tf_op jit(solution)/shard_map/all_to_all | solution.py:35
  195.4 19.5 %copy-start.11 = (bf16[1,64,7168]{2,1,0:T(8,128)(2,1)S(1)}, bf16[1,64,7168]{2,1,0:T(8,128)(2,1)}, u32[]{:S(2)}) copy-start(bf16[1,64,7168]{2,1,0:T(8,128)(2,1)} %param.8) | copy-start | bytes 2752516
  198.4 42.8 %copy-start.15 = (f32[1,7168]{1,0:T(1,128)S(1)}, f32[1,7168]{1,0:T(1,128)}, u32[]{:S(2)}) copy-start(f32[1,7168]{1,0:T(1,128)} %gain.3) | copy-start | bytes 86020
  198.4 35.8 %collective-permute-start.3 = (bf16[64,7168]{1,0:T(8,128)(2,1)S(1)}, bf16[64,7168]{1,0:T(8,128)(2,1)S(1)}, u32[]{:S(2)}, u32[]{:S(2)}) collective-permute-start(bf16[64,7168]{1,0:T(8,128)(2,1)S(1)} %shard_map.89), channel_id=1, source_target_pairs={{0,32},{32,64},{64,96},{96,128},{128,160},{160,192},{192,224},{224... | collective-permute-start | bytes 2752520 | tf_op jit(solution)/shard_map/ppermute | solution.py:26
  217.7 23.4 %collective-permute-start.4 = (bf16[64,7168]{1,0:T(8,128)(2,1)S(1)}, bf16[64,7168]{1,0:T(8,128)(2,1)S(1)}, u32[]{:S(2)}, u32[]{:S(2)}) collective-permute-start(bf16[64,7168]{1,0:T(8,128)(2,1)S(1)} %shard_map.90), channel_id=1, source_target_pairs={{0,224},{32,0},{64,32},{96,64},{128,96},{160,128},{192,160},{224,1... | collective-permute-start | bytes 2752520 | tf_op jit(solution)/shard_map/ppermute | solution.py:26
  242.3 0.9 copy-start.12
  243.2 91.8 %copy-start.1 = (bf16[3584,256]{1,0:T(8,128)(2,1)S(1)}, bf16[3584,256]{1,0:T(8,128)(2,1)}, u32[]{:S(2)}) copy-start(bf16[3584,256]{1,0:T(8,128)(2,1)} %get-tuple-element.5.kept) | copy-start | bytes 5505028
  243.2 91.8 %copy-start.7 = (bf16[3584,256]{1,0:T(8,128)(2,1)S(1)}, bf16[3584,256]{1,0:T(8,128)(2,1)}, u32[]{:S(2)}) copy-start(bf16[3584,256]{1,0:T(8,128)(2,1)} %copy-done.5) | copy-start | bytes 5505028
  337.1 3.3 collective-permute-start.5
  343.9 1.8 copy-start.3
  345.8 90.2 %copy-start.13 = (bf16[64,7168]{1,0:T(8,128)(2,1)S(1)}, bf16[64,7168]{1,0:T(8,128)(2,1)}, u32[]{:S(2)}) copy-start(bf16[64,7168]{1,0:T(8,128)(2,1)} %copy-done.12) | copy-start | bytes 2752516
  345.8 90.2 %all-to-all-start.3 = ((bf16[32,16,3584]{2,1,0:T(8,128)(2,1)}), bf16[32,16,3584]{2,1,0:T(8,128)(2,1)}, u32[]{:S(2)}, u32[]{:S(2)}) async-start(bf16[32,16,3584]{2,1,0:T(8,128)(2,1)} %bitcast.35), calls=%async_computation.3 | async-start | bytes 7340032 | tf_op jit(solution)/shard_map/all_to_all | solution.py:35

commit v3 on v2

--- a/solution.py
+++ b/solution.py
@@ -13,7 +13,8 @@
 HALVES = SPLIT // CORES
 COURSES = 2
 TILE = 512
-VMEM_BYTES = 20 * 1024 * 1024
+SMALL = 20 * 1024 * 1024
+LARGE = 56 * 1024 * 1024
 
 epsilon = 1e-06
 
@@ -35,14 +36,8 @@
     return lax.all_to_all(blocks, "expert", split_axis=0, concat_axis=0, tiled=True)
 
 
-def kernel_call(body, shape, dtype, *operands):
-    return pl.pallas_call(
-        body,
-        out_shape=jax.ShapeDtypeStruct(shape, dtype),
-        in_specs=[pl.BlockSpec(memory_space=pltpu.VMEM)] * len(operands),
-        out_specs=pl.BlockSpec(memory_space=pltpu.VMEM),
-        compiler_params=pltpu.CompilerParams(vmem_limit_bytes=VMEM_BYTES),
-    )(*operands)
+def params(limit):
+    return pltpu.CompilerParams(vmem_limit_bytes=limit)
 
 
 def tiles(width):
@@ -63,6 +58,12 @@
     return (iota((experts * capacity, tokens), 0) == route * capacity + position).astype(BF16)
 
 
+def column(line):
+    size = line.shape[1]
+    same = iota((size, size), 0) == iota((size, size), 1)
+    return jnp.sum(jnp.where(same, line, jnp.zeros_like(line)), axis=1, keepdims=True)
+
+
 def tokens_by_slots(route, experts, capacity):
     tokens = route.shape[0]
     chosen = (iota((tokens, experts), 1) == route).astype(F32)
@@ -72,7 +73,7 @@
     return (iota((tokens, experts * capacity), 1) == route * capacity + position).astype(BF16)
 
 
-def prepare_body(experts, capacity, first, second, gain, routes, out):
+def prepare_body(experts, capacity, moment, first, second, gain, routes, out, slotted, sems):
     width = first.shape[1]
     part = width // CORES
     states = (first, second)
@@ -83,7 +84,8 @@
             piece = state[:, low:high].astype(F32)
             total = total + jnp.sum(piece * piece, axis=1, keepdims=True)
         scales.append(lax.rsqrt(total / width + epsilon))
-        tables.append(slots_by_tokens(routes[course : course + 1, :], experts, capacity))
+        tables.append(slots_by_tokens(routes[course, moment], experts, capacity))
+    copies = []
     for core in range(CORES):
         for low, high in tiles(part):
             columns = slice(core * part + low, core * part + high)
@@ -94,14 +96,86 @@
             for e in range(experts):
                 span = slice(e * capacity, (e + 1) * capacity)
                 block = jnp.concatenate([r[span] for r in rows], axis=0).astype(BF16)
-                for half in range(HALVES):
-                    out[e * SPLIT + half * CORES + core, :, low:high] = block
+                slotted[core, e, :, low:high] = block
+        for half in range(HALVES):
+            copy = pltpu.make_async_copy(
+                slotted.at[core], out.at[:, half, core], sems.at[core, half]
+            )
+            copy.start()
+            copies.append(copy)
+    for copy in copies:
+        copy.wait()
+
+
+def prepare(states, gain, routes, experts, capacity, moment, limit):
+    part = states[0].shape[1] // CORES
+    rows = COURSES * capacity
+    return pl.pallas_call(
+        functools.partial(prepare_body, experts, capacity, moment),
+        out_shape=jax.ShapeDtypeStruct((experts, HALVES, CORES, rows, part), BF16),
+        in_specs=[pl.BlockSpec(memory_space=pltpu.VMEM)] * 4,
+        out_specs=pl.BlockSpec(memory_space=pl.ANY),
+        scratch_shapes=[
+            pltpu.VMEM((CORES, experts, rows, part), BF16),
+            pltpu.SemaphoreType.DMA((CORES, HALVES)),
+        ],
+        compiler_params=params(limit),
+    )(*states, gain, routes)
+
+
+def started(pairs, sems):
+    copies = [pltpu.make_async_copy(*pair, sems.at[i]) for i, pair in enumerate(pairs)]
+    for copy in copies:
+        copy.start()
+    return copies
+
+
+def streamed_up_body(rows, kept, got, out, rows_held, kept_held, got_held, sems):
+    hidden = kept.shape[1]
+    bounds = tiles(rows.shape[1])
+    pairs = []
+    for low, high in bounds:
+        span = slice(low, high)
+        pairs.append((kept.at[span], kept_held.at[span]))
+        pairs.append((got.at[span], got_held.at[span]))
+        pairs.append((rows.at[:, span], rows_held.at[:, span]))
+    copies = started(pairs, sems)
+    for i, (low, high) in enumerate(bounds):
+        for copy in copies[3 * i : 3 * i + 3]:
+            copy.wait()
+        piece = rows_held[:, low:high]
+        mine = jnp.dot(piece, kept_held[low:high], preferred_element_type=F32)
+        other = jnp.dot(piece, got_held[low:high], preferred_element_type=F32)
+        if i == 0:
+            out[:, :hidden] = mine
+            out[:, hidden:] = other
+        else:
+            out[:, :hidden] += mine
+            out[:, hidden:] += other
 
 
 def up_body(rows, kept, got, out):
     hidden = kept.shape[1]
     out[:, :hidden] = jnp.dot(rows[...], kept[...], preferred_element_type=F32)
     out[:, hidden:] = jnp.dot(rows[...], got[...], preferred_element_type=F32)
+
+
+def up(rows, kept, got, streamed):
+    count, part = rows.shape
+    scratch = [
+        pltpu.VMEM(rows.shape, BF16),
+        pltpu.VMEM(kept.shape, BF16),
+        pltpu.VMEM(got.shape, BF16),
+        pltpu.SemaphoreType.DMA((3 * len(tiles(part)),)),
+    ]
+    return pl.pallas_call(
+        streamed_up_body if streamed else up_body,
+        out_shape=jax.ShapeDtypeStruct((count, CORES * kept.shape[1]), F32),
+        in_specs=[pl.BlockSpec(memory_space=pl.ANY if streamed else pltpu.VMEM)] * 3,
+        out_specs=pl.BlockSpec(memory_space=pltpu.VMEM),
+        scratch_shapes=scratch if streamed else [],
+        compiler_params=params(LARGE if streamed else SMALL),
+    )(rows, kept, got)
 
 
 def down_body(mine, theirs, kept, got, out):
@@ -114,24 +188,70 @@
         out[:, low:high] = total.astype(out.dtype)
 
 
-def finish_body(experts, capacity, course, state, returned, route, gate, out):
-    width = state.shape[1]
-    part = width // CORES
-    table = tokens_by_slots(route[...], experts, capacity)
-    span = slice(course * capacity, (course + 1) * capacity)
-    for core in range(CORES):
-        for low, high in tiles(part):
+def down(mine, theirs, kept, got):
+    return pl.pallas_call(
+        down_body,
+        out_shape=jax.ShapeDtypeStruct((mine.shape[0], kept.shape[1]), BF16),
+        in_specs=[pl.BlockSpec(memory_space=pltpu.VMEM)] * 4,
+        out_specs=pl.BlockSpec(memory_space=pltpu.VMEM),
+        compiler_params=params(SMALL),
+    )(mine, theirs, kept, got)
+
+
+def finish_body(
+    capacity, moment, first, second, returned, routes, gates, new_first, new_second, held, sems
+):
+    experts = returned.shape[0]
+    part = returned.shape[-1]
+    step = part // 2
+    spans = [(core, low) for core in range(CORES) for low in (0, step)]
+    copies = started(
+        [
+            (
+                returned.at[:, :, core, :, low : low + step],
+                held.at[:, :, core, :, low : low + step],
+            )
+            for core, low in spans
+        ],
+        sems,
+    )
+    chosen = [column(routes[course, moment]) for course in range(COURSES)]
+    tables = [tokens_by_slots(route, experts, capacity) for route in chosen]
+    scales = [column(gates[course, moment]) for course in range(COURSES)]
+    for copy, (core, start) in zip(copies, spans):
+        copy.wait()
+        for low in range(start, start + step, TILE // 2):
+            high = low + TILE // 2
+            summed = [
+                held[e, 0, core, :, low:high].astype(F32)
+                + held[e, 1, core, :, low:high].astype(F32)
+                for e in range(experts)
+            ]
             columns = slice(core * part + low, core * part + high)
-            produced = []
-            for e in range(experts):
-                blocks = [
-                    returned[e * SPLIT + half * CORES + core, :, low:high].astype(F32)[span]
-                    for half in range(HALVES)
-                ]
-                produced.append(sum(blocks))
-            produced = jnp.concatenate(produced, axis=0).astype(BF16)
-            gathered = jnp.dot(table, produced, preferred_element_type=F32)
-            out[:, columns] = (state[:, columns].astype(F32) + gathered * gate[...]).astype(BF16)
+            for course, (state, new) in enumerate(((first, new_first), (second, new_second))):
+                span = slice(course * capacity, (course + 1) * capacity)
+                produced = jnp.concatenate([block[span] for block in summed], axis=0)
+                gathered = jnp.dot(
+                    tables[course], produced.astype(BF16), preferred_element_type=F32
+                )
+                new[:, columns] = (
+                    state[:, columns].astype(F32) + gathered * scales[course]
+                ).astype(BF16)
+
+
+def finish(states, returned, routes, gates, experts, capacity, moment):
+    tokens, width = states[0].shape
+    rows, part = returned.shape[-2:]
+    shape = (experts, HALVES, CORES, rows, part)
+    vmem = pl.BlockSpec(memory_space=pltpu.VMEM)
+    return pl.pallas_call(
+        functools.partial(finish_body, capacity, moment),
+        out_shape=[jax.ShapeDtypeStruct((tokens, width), BF16)] * COURSES,
+        in_specs=[vmem, vmem, pl.BlockSpec(memory_space=pl.ANY), vmem, vmem],
+        out_specs=[vmem] * COURSES,
+        scratch_shapes=[pltpu.VMEM(shape, BF16), pltpu.SemaphoreType.DMA((2 * CORES,))],
+        compiler_params=params(SMALL),
+    )(*states, returned.reshape(shape), routes, gates)
 
 
 def per_device(
@@ -143,7 +263,6 @@
     tokens, width = states[0].shape
     capacity = tokens // experts
     part = width // CORES
-    hidden = up_weight.shape[-1]
     block = (devices, COURSES * capacity, part)
 
     core = lax.axis_index("expert") % CORES
@@ -153,33 +272,18 @@
     up_kept = lax.dynamic_slice_in_dim(up_own, core * part, part, 0)
     down_kept = lax.dynamic_slice_in_dim(down_own, core * part, part, 1)
 
+    lines = (COURSES, STEPS, 1, tokens)
+    routes, gates = routes.reshape(lines), gate_values.reshape(lines)
     for t in range(STEPS):
-        sending = kernel_call(
-            functools.partial(prepare_body, experts, capacity),
-            block,
-            BF16,
-            *states,
-            norm_gain,
-            routes[0, :, t, :, 0],
-        )
-        rows = exchange(sending).reshape(-1, part)
-        sums = kernel_call(up_body, (rows.shape[0], hidden * CORES), F32, rows, up_kept, up_got)
-        partial = kernel_call(
-            down_body, rows.shape, BF16, sums, across_cores(sums), down_kept, down_got
-        )
+        limit = LARGE if t == 0 else SMALL
+        sending = prepare(states, norm_gain, routes, experts, capacity, t, limit)
+        rows = exchange(sending.reshape(block)).reshape(-1, part)
+        sums = up(rows, up_kept, up_got, t == 0)
+        partial = down(sums, across_cores(sums), down_kept, down_got)
         returned = exchange(partial.reshape(block))
-        for c in range(COURSES):
-            states[c] = kernel_call(
-                functools.partial(finish_body, experts, capacity, c),
-                (tokens, width),
-                BF16,
-                states[c],
-                returned,
-                routes[0, c, t],
-                gate_values[0, c, t],
-            )
-            if t + 1 < STEPS:
-                states[c] = passed_along(states[c], "section", 1 - 2 * c)
+        states = finish(states, returned, routes, gates, experts, capacity, t)
+        if t + 1 < STEPS:
+            states = [passed_along(states[c], "section", 1 - 2 * c) for c in range(COURSES)]
     return (states[0][None], states[1][None])
 
 

time: 444 us -> 428 us (0.964)
  blocking collectives: 91.8 us -> 254 us
  waiting for transfers between devices: 258 us -> 104 us
  local copies, waits for them, and re-layouts: 20.5 us -> 6.48 us
  starting transfers between devices: 43.1 us -> 35.5 us
    all_to_all x1 -> x3, blocking collectives: 91.8 us -> 254 us  [exchange(): lax.all_to_all(blocks, 'expert', split_axis=0, concat_axis=0, tiled=True)]
    all_to_all x3 -> x1, waiting for transfers between devices: 229 us -> 73.6 us  [exchange(): lax.all_to_all(blocks, 'expert', split_axis=0, concat_axis=0, tiled=True)]
    unnamed x38 -> x16, local copies, waits for them, and re-layouts: 13.8 us -> 1.26 us
    all_to_all x3 -> x1, starting transfers between devices: 21.8 us -> 12 us  [exchange(): lax.all_to_all(blocks, 'expert', split_axis=0, concat_axis=0, tiled=True)]
    pallas_call x10 -> x8, Pallas kernels: 28.8 us -> 25.9 us  [the longest x2 8.33 us: up(): pl.pallas_call(streamed_up_body if streamed else up_body, out_shape=jax.S...]
  transfers between devices with their start and end apart: 9 -> 7, of which waited for: 8 -> 6; matrix products, arithmetic and copies ran while one was open for 1% -> 1% of each run, Pallas kernels for 2% -> 1%
where the time goes in v3:
time: 428 us; the launch traced here: 427 us
  blocking collectives  254 us (59%)
  waiting for transfers between devices  104 us (24%)
  starting transfers between devices  35.5 us (8%)
  Pallas kernels  25.9 us (6%)
  local copies, waits for them, and re-layouts  6.48 us (2%)
    all_to_all x3, blocking collectives, exchange(): lax.all_to_all(blocks, 'expert', split_axis=0, concat_axis=0, tiled=True)  254 us
    all_to_all x1, waiting for transfers between devices, exchange(): lax.all_to_all(blocks, 'expert', split_axis=0, concat_axis=0, tiled=True)  73.6 us
    ppermute x2, waiting for transfers between devices, passed_along(): lax.ppermute(array, axis, [(i, (i + by) % size) for i in range(size)])  23.6 us
    ppermute x2, starting transfers between devices, passed_along(): lax.ppermute(array, axis, [(i, (i + by) % size) for i in range(size)])  19.2 us
    all_to_all x1, starting transfers between devices, exchange(): lax.all_to_all(blocks, 'expert', split_axis=0, concat_axis=0, tiled=True)  12 us
  transfers between devices with their start and end apart: 7, of which 6 were waited for; matrix products, arithmetic and copies ran while one was open for 1% of the time, Pallas kernels for 1%

profile of v3, /device:TPU:7, one launch (start us, length us, event | category | flops | bytes accessed | tf_op | source)
XLA Modules:
  0.0 427.0 jit_solution(17974911286666479915)
XLA Ops:
  0.6 4.1 shard_map.86
  4.8 12.0 %all-to-all-start = ((bf16[32,16,3584]{2,1,0:T(8,128)(2,1)}), bf16[32,16,3584]{2,1,0:T(8,128)(2,1)}, u32[]{:S(2)}, u32[]{:S(2)}) async-start(bf16[32,16,3584]{2,1,0:T(8,128)(2,1)} %bitcast.38), calls=%async_computation | async-start | bytes 7340032 | tf_op jit(solution)/shard_map/all_to_all | solution.py:36
  16.8 0.0 copy-start.7
  16.8 3.8 dynamic-slice_bitcast_fusion.2
  20.6 0.3 collective-permute-start
  20.9 0.0 copy-done.7
  20.9 1.5 dynamic-slice_bitcast_fusion
  22.3 0.2 collective-permute-start.2
  22.5 1.9 collective-permute-done.got
  24.5 73.6 %all-to-all-done = bf16[32,16,3584]{2,1,0:T(8,128)(2,1)} async-done(((bf16[32,16,3584]{2,1,0:T(8,128)(2,1)}), bf16[32,16,3584]{2,1,0:T(8,128)(2,1)}, u32[]{:S(2)}, u32[]{:S(2)}) %all-to-all-start) | async-done | bytes 3670048 | tf_op jit(solution)/shard_map/all_to_all | solution.py:36
  98.0 4.8 %shard_map.87.mine = f32[512,512]{1,0:T(8,128)} custom-call(bf16[512,3584]{1,0:T(8,128)(2,1)} %bitcast.4.rows, bf16[3584,256]{1,0:T(8,128)(2,1)} %get-tuple-element.13.kept, bf16[3584,256]{1,0:T(8,128)(2,1)} %collective-permute-done.got), custom_call_target="tpu_custom_call" | custom-call | tf_op jit(solution)/shard_map/pallas_call | solution.py:171
  102.8 2.7 collective-permute-start.1
  105.5 0.0 collective-permute-done.2.got
  105.5 2.5 collective-permute-done.1.theirs
  108.0 0.0 copy-start.1
  108.0 1.2 copy-done.1
  109.3 3.6 shard_map.88
  112.9 0.0 copy-start.2
  112.9 0.0 copy-start.3
  112.9 0.0 copy-start.5
  112.9 0.0 copy-start.6
  112.9 74.0 %all_to_all.20 = bf16[32,16,3584]{2,1,0:T(8,128)(2,1)S(1)} all-to-all(bf16[32,16,3584]{2,1,0:T(8,128)(2,1)S(1)} %bitcast.23), channel_id=1, replica_groups=mesh['section'=8,'expert'=32] {'expert'}, dimensions={0} | all-to-all | bytes 7340032 | tf_op jit(solution)/shard_map/all_to_all | solution.py:36
  186.9 0.0 copy-start.4
  186.9 0.0 copy-done.2
  186.9 0.0 copy-done.3
  186.9 0.0 copy-done.5
  187.0 0.0 copy-done.6
  187.0 1.7 shard_map.89
  188.7 19.2 %collective-permute-start.3 = (bf16[64,7168]{1,0:T(8,128)(2,1)S(1)}, bf16[64,7168]{1,0:T(8,128)(2,1)S(1)}, u32[]{:S(2)}, u32[]{:S(2)}) collective-permute-start(bf16[64,7168]{1,0:T(8,128)(2,1)S(1)} %get-tuple-element.6), channel_id=1, source_target_pairs={{0,32},{32,64},{64,96},{96,128},{128,160},{160,192},{192,224},{224... | collective-permute-start | bytes 2752520 | tf_op jit(solution)/shard_map/ppermute | solution.py:27
  207.9 0.0 collective-permute-start.4
  207.9 19.6 %collective-permute-done.3.first = bf16[64,7168]{1,0:T(8,128)(2,1)S(1)} collective-permute-done((bf16[64,7168]{1,0:T(8,128)(2,1)S(1)}, bf16[64,7168]{1,0:T(8,128)(2,1)S(1)}, u32[]{:S(2)}, u32[]{:S(2)}) %collective-permute-start.3) | collective-permute-done | bytes 917536 | tf_op jit(solution)/shard_map/ppermute | solution.py:27
  227.5 4.0 collective-permute-done.4.second
  231.5 0.0 copy-done.4
  231.5 1.6 shard_map.90
  233.1 0.0 copy-start
  233.1 90.2 %all_to_all.21 = bf16[32,16,3584]{2,1,0:T(8,128)(2,1)S(1)} all-to-all(bf16[32,16,3584]{2,1,0:T(8,128)(2,1)S(1)} %bitcast.27), channel_id=1, replica_groups=mesh['section'=8,'expert'=32] {'expert'}, dimensions={0} | all-to-all | bytes 7340032 | tf_op jit(solution)/shard_map/all_to_all | solution.py:36
  323.3 0.0 copy-done
  323.3 3.6 shard_map.91.mine
  326.8 1.1 collective-permute-start.5
  327.9 2.3 collective-permute-done.5.theirs
  330.2 3.6 shard_map.92
  333.8 90.0 %all_to_all.22 = bf16[32,16,3584]{2,1,0:T(8,128)(2,1)S(1)} all-to-all(bf16[32,16,3584]{2,1,0:T(8,128)(2,1)S(1)} %bitcast.22), channel_id=1, replica_groups=mesh['section'=8,'expert'=32] {'expert'}, dimensions={0} | all-to-all | bytes 7340032 | tf_op jit(solution)/shard_map/all_to_all | solution.py:36
  423.9 3.0 shard_map.93
Async XLA Ops:
  4.8 93.2 %all-to-all-start = ((bf16[32,16,3584]{2,1,0:T(8,128)(2,1)}), bf16[32,16,3584]{2,1,0:T(8,128)(2,1)}, u32[]{:S(2)}, u32[]{:S(2)}) async-start(bf16[32,16,3584]{2,1,0:T(8,128)(2,1)} %bitcast.38), calls=%async_computation | async-start | bytes 7340032 | tf_op jit(solution)/shard_map/all_to_all | solution.py:36
  16.8 4.1 copy-start.7
  20.6 3.9 collective-permute-start
  22.3 83.2 %collective-permute-start.2 = (bf16[256,3584]{1,0:T(8,128)(2,1)}, bf16[256,3584]{1,0:T(8,128)(2,1)}, u32[]{:S(2)}, u32[]{:S(2)}) collective-permute-start(bf16[256,3584]{1,0:T(8,128)(2,1)} %get-tuple-element.10), channel_id=1, source_target_pairs={{0,1},{1,0},{2,3},{3,2},{4,5},{5,4},{6,7},{7,6},{8,9},{9,8},{10,11... | collective-permute-start | bytes 5505032 | tf_op jit(solution)/shard_map/ppermute | solution.py:32
  102.8 5.2 %collective-permute-start.1 = (f32[512,512]{1,0:T(8,128)}, f32[512,512]{1,0:T(8,128)S(1)}, u32[]{:S(2)}, u32[]{:S(2)}) collective-permute-start(f32[512,512]{1,0:T(8,128)} %shard_map.87.mine), channel_id=1, source_target_pairs={{0,1},{1,0},{2,3},{3,2},{4,5},{5,4},{6,7},{7,6},{8,9},{9,8},{10,11... | collective-permute-start | bytes 3145736 | tf_op jit(solution)/shard_map/ppermute | solution.py:32
  108.0 1.2 copy-start.1
  112.9 74.1 %copy-start.2 = (bf16[1,64,7168]{2,1,0:T(8,128)(2,1)S(1)}, bf16[1,64,7168]{2,1,0:T(8,128)(2,1)}, u32[]{:S(2)}) copy-start(bf16[1,64,7168]{2,1,0:T(8,128)(2,1)} %param.7) | copy-start | bytes 2752516
  112.9 74.1 %copy-start.3 = (bf16[1,64,7168]{2,1,0:T(8,128)(2,1)S(1)}, bf16[1,64,7168]{2,1,0:T(8,128)(2,1)}, u32[]{:S(2)}) copy-start(bf16[1,64,7168]{2,1,0:T(8,128)(2,1)} %param.8) | copy-start | bytes 2752516
  112.9 74.1 %copy-start.5 = (s32[1,2,2,64,1]{3,4,2,1,0:T(1,128)S(1)}, s32[1,2,2,64,1]{3,4,2,1,0:T(1,128)}, u32[]{:S(2)}) copy-start(s32[1,2,2,64,1]{3,4,2,1,0:T(1,128)} %param.10) | copy-start | bytes 3076
  112.9 74.1 %copy-start.6 = (f32[1,2,2,64,1]{3,4,2,1,0:T(1,128)S(1)}, f32[1,2,2,64,1]{3,4,2,1,0:T(1,128)}, u32[]{:S(2)}) copy-start(f32[1,2,2,64,1]{3,4,2,1,0:T(1,128)} %param.11) | copy-start | bytes 3076
  186.9 44.6 %copy-start.4 = (f32[1,7168]{1,0:T(1,128)S(1)}, f32[1,7168]{1,0:T(1,128)}, u32[]{:S(2)}) copy-start(f32[1,7168]{1,0:T(1,128)} %gain.3) | copy-start | bytes 86020
  188.7 38.8 %collective-permute-start.3 = (bf16[64,7168]{1,0:T(8,128)(2,1)S(1)}, bf16[64,7168]{1,0:T(8,128)(2,1)S(1)}, u32[]{:S(2)}, u32[]{:S(2)}) collective-permute-start(bf16[64,7168]{1,0:T(8,128)(2,1)S(1)} %get-tuple-element.6), channel_id=1, source_target_pairs={{0,32},{32,64},{64,96},{96,128},{128,160},{160,192},{192,224},{224... | collective-permute-start | bytes 2752520 | tf_op jit(solution)/shard_map/ppermute | solution.py:27
  207.9 23.6 %collective-permute-start.4 = (bf16[64,7168]{1,0:T(8,128)(2,1)S(1)}, bf16[64,7168]{1,0:T(8,128)(2,1)S(1)}, u32[]{:S(2)}, u32[]{:S(2)}) collective-permute-start(bf16[64,7168]{1,0:T(8,128)(2,1)S(1)} %get-tuple-element.7), channel_id=1, source_target_pairs={{0,224},{32,0},{64,32},{96,64},{128,96},{160,128},{192,160},{224,1... | collective-permute-start | bytes 2752520 | tf_op jit(solution)/shard_map/ppermute | solution.py:27
  233.1 90.2 %copy-start = (bf16[3584,256]{1,0:T(8,128)(2,1)S(1)}, bf16[3584,256]{1,0:T(8,128)(2,1)}, u32[]{:S(2)}) copy-start(bf16[3584,256]{1,0:T(8,128)(2,1)} %get-tuple-element.13.kept) | copy-start | bytes 5505028
  326.8 3.4 collective-permute-start.5

commit v4 on v3

--- a/solution.py
+++ b/solution.py
@@ -130,6 +130,23 @@
     return copies
 
 
+def hold_body(*refs):
+    half = (len(refs) - 1) // 2
+    for copy in started(list(zip(refs[:half], refs[half:-1])), refs[-1]):
+        copy.wait()
+
+
+def hold(*arrays):
+    return pl.pallas_call(
+        hold_body,
+        out_shape=[pltpu.VMEM(x.shape, x.dtype) for x in arrays],
+        in_specs=[pl.BlockSpec(memory_space=pl.ANY)] * len(arrays),
+        out_specs=[pl.BlockSpec(memory_space=pltpu.VMEM)] * len(arrays),
+        scratch_shapes=[pltpu.SemaphoreType.DMA((len(arrays),))],
+        compiler_params=params(SMALL),
+    )(*arrays)
+
+
 def streamed_up_body(rows, kept, got, out, rows_held, kept_held, got_held, sems):
     hidden = kept.shape[1]
     bounds = tiles(rows.shape[1])
@@ -170,7 +187,7 @@
     ]
     return pl.pallas_call(
         streamed_up_body if streamed else up_body,
-        out_shape=jax.ShapeDtypeStruct((count, CORES * kept.shape[1]), F32),
+        out_shape=pltpu.VMEM((count, CORES * kept.shape[1]), F32),
         in_specs=[pl.BlockSpec(memory_space=pl.ANY if streamed else pltpu.VMEM)] * 3,
         out_specs=pl.BlockSpec(memory_space=pltpu.VMEM),
         scratch_shapes=scratch if streamed else [],
@@ -272,18 +289,23 @@
     up_kept = lax.dynamic_slice_in_dim(up_own, core * part, part, 0)
     down_kept = lax.dynamic_slice_in_dim(down_own, core * part, part, 1)
 
+    near_down = hold(down_kept, down_got)
     lines = (COURSES, STEPS, 1, tokens)
     routes, gates = routes.reshape(lines), gate_values.reshape(lines)
     for t in range(STEPS):
         limit = LARGE if t == 0 else SMALL
         sending = prepare(states, norm_gain, routes, experts, capacity, t, limit)
         rows = exchange(sending.reshape(block)).reshape(-1, part)
-        sums = up(rows, up_kept, up_got, t == 0)
-        partial = down(sums, across_cores(sums), down_kept, down_got)
+        rows, near_down = lax.optimization_barrier((rows, near_down))
+        sums = up(rows, up_kept, up_got, True) if t == 0 else up(rows, *near_up, False)
+        partial = down(sums, across_cores(sums), *near_down)
         returned = exchange(partial.reshape(block))
         states = finish(states, returned, routes, gates, experts, capacity, t)
         if t + 1 < STEPS:
+            up_kept, up_got, *states = lax.optimization_barrier((up_kept, up_got, *states))
+            near_up = hold(up_kept, up_got)
             states = [passed_along(states[c], "section", 1 - 2 * c) for c in range(COURSES)]
+            states, near_up = lax.optimization_barrier((states, near_up))
     return (states[0][None], states[1][None])
 
 

time: 428 us -> 420 us (0.981)
  transfers between devices with their start and end apart: 7 -> 7, of which waited for: 6 -> 6; matrix products, arithmetic and copies ran while one was open for 1% -> 1% of each run, Pallas kernels for 1% -> 0%
where the time goes in v4:
time: 420 us
  blocking collectives  254 us (60%)
  waiting for transfers between devices  101 us (24%)
  starting transfers between devices  35.6 us (8%)
  Pallas kernels  22.5 us (5%)
  local copies, waits for them, and re-layouts  6.09 us (1%)
    all_to_all x3, blocking collectives, exchange(): lax.all_to_all(blocks, 'expert', split_axis=0, concat_axis=0, tiled=True)  254 us
    all_to_all x1, waiting for transfers between devices, exchange(): lax.all_to_all(blocks, 'expert', split_axis=0, concat_axis=0, tiled=True)  73.4 us
    ppermute x2, waiting for transfers between devices, passed_along(): lax.ppermute(array, axis, [(i, (i + by) % size) for i in range(size)])  21.9 us
    ppermute x2, starting transfers between devices, passed_along(): lax.ppermute(array, axis, [(i, (i + by) % size) for i in range(size)])  19.2 us
    all_to_all x1, starting transfers between devices, exchange(): lax.all_to_all(blocks, 'expert', split_axis=0, concat_axis=0, tiled=True)  12 us
  transfers between devices with their start and end apart: 7, of which 6 were waited for; matrix products, arithmetic and copies ran while one was open for 1% of the time, Pallas kernels for 0%

profile of v4, /device:TPU:7, one launch (start us, length us, event | category | flops | bytes accessed | tf_op | source)
XLA Modules:
  0.0 419.7 jit_solution(8630387408949241423)
XLA Ops:
  0.6 4.2 shard_map.86
  4.8 12.0 %all-to-all-start = ((bf16[32,16,3584]{2,1,0:T(8,128)(2,1)}), bf16[32,16,3584]{2,1,0:T(8,128)(2,1)}, u32[]{:S(2)}, u32[]{:S(2)}) async-start(bf16[32,16,3584]{2,1,0:T(8,128)(2,1)} %bitcast.38), calls=%async_computation | async-start | bytes 7340032 | tf_op jit(solution)/shard_map/all_to_all | solution.py:36
  16.8 0.0 copy-start.8
  16.8 2.4 dynamic-slice_bitcast_fusion
  19.3 0.4 collective-permute-start.1
  19.7 0.3 copy-done.8
  20.0 2.1 dynamic-slice_bitcast_fusion.2
  22.1 0.3 collective-permute-start
  22.4 0.8 collective-permute-done.1.refs_1_
  23.1 0.3 shard_map.87
  23.4 0.0 copy-start.1
  23.4 1.2 copy-done.1
  24.6 73.4 %all-to-all-done = bf16[32,16,3584]{2,1,0:T(8,128)(2,1)} async-done(((bf16[32,16,3584]{2,1,0:T(8,128)(2,1)}), bf16[32,16,3584]{2,1,0:T(8,128)(2,1)}, u32[]{:S(2)}, u32[]{:S(2)}) %all-to-all-start) | async-done | bytes 3670048 | tf_op jit(solution)/shard_map/all_to_all | solution.py:36
  98.0 0.0 collective-permute-done.got.refs_1_
  98.0 0.0 copy-start.2
  98.1 3.9 shard_map.88.mine
  102.0 2.7 collective-permute-start.2
  104.7 2.3 collective-permute-done.2.theirs
  107.0 0.0 copy-done.2
  107.0 2.1 shard_map.89
  109.1 0.0 copy-start.3
  109.1 0.0 copy-start.4
  109.1 0.0 copy-start.6
  109.2 0.0 copy-start.7
  109.2 74.0 %all_to_all.20 = bf16[32,16,3584]{2,1,0:T(8,128)(2,1)S(1)} all-to-all(bf16[32,16,3584]{2,1,0:T(8,128)(2,1)S(1)} %bitcast.23), channel_id=1, replica_groups=mesh['section'=8,'expert'=32] {'expert'}, dimensions={0} | all-to-all | bytes 7340032 | tf_op jit(solution)/shard_map/all_to_all | solution.py:36
  183.2 0.0 copy-done.3
  183.2 0.0 copy-done.4
  183.2 0.0 copy-done.6
  183.2 0.0 copy-done.7
  183.2 0.0 copy-start
  183.2 1.7 shard_map.90
  185.0 0.0 copy-start.5
  185.0 19.2 %collective-permute-start.3 = (bf16[64,7168]{1,0:T(8,128)(2,1)S(1)}, bf16[64,7168]{1,0:T(8,128)(2,1)S(1)}, u32[]{:S(2)}, u32[]{:S(2)}) collective-permute-start(bf16[64,7168]{1,0:T(8,128)(2,1)S(1)} %get-tuple-element.31), channel_id=1, source_target_pairs={{0,32},{32,64},{64,96},{96,128},{128,160},{160,192},{192,224},{224... | collective-permute-start | bytes 2752520 | tf_op jit(solution)/shard_map/ppermute | solution.py:27
  204.2 0.0 collective-permute-start.4
  204.2 0.0 copy-done
  204.2 1.6 shard_map.91
  205.9 17.9 %collective-permute-done.3.first = bf16[64,7168]{1,0:T(8,128)(2,1)S(1)} collective-permute-done((bf16[64,7168]{1,0:T(8,128)(2,1)S(1)}, bf16[64,7168]{1,0:T(8,128)(2,1)S(1)}, u32[]{:S(2)}, u32[]{:S(2)}) %collective-permute-start.3) | collective-permute-done | bytes 917536 | tf_op jit(solution)/shard_map/ppermute | solution.py:27
  223.8 4.0 collective-permute-done.4.second
  227.8 0.0 copy-done.5
  227.8 1.6 shard_map.92
  229.4 90.2 %all_to_all.21 = bf16[32,16,3584]{2,1,0:T(8,128)(2,1)S(1)} all-to-all(bf16[32,16,3584]{2,1,0:T(8,128)(2,1)S(1)} %bitcast.27), channel_id=1, replica_groups=mesh['section'=8,'expert'=32] {'expert'}, dimensions={0} | all-to-all | bytes 7340032 | tf_op jit(solution)/shard_map/all_to_all | solution.py:36
  319.5 2.1 shard_map.93.mine
  321.6 0.9 collective-permute-start.5
  322.5 2.3 collective-permute-done.5.theirs
  324.8 2.1 shard_map.94
  326.9 89.7 %all_to_all.22 = bf16[32,16,3584]{2,1,0:T(8,128)(2,1)S(1)} all-to-all(bf16[32,16,3584]{2,1,0:T(8,128)(2,1)S(1)} %bitcast.22), channel_id=1, replica_groups=mesh['section'=8,'expert'=32] {'expert'}, dimensions={0} | all-to-all | bytes 7340032 | tf_op jit(solution)/shard_map/all_to_all | solution.py:36
  416.6 3.0 shard_map.95
Async XLA Ops:
  4.8 93.2 %all-to-all-start = ((bf16[32,16,3584]{2,1,0:T(8,128)(2,1)}), bf16[32,16,3584]{2,1,0:T(8,128)(2,1)}, u32[]{:S(2)}, u32[]{:S(2)}) async-start(bf16[32,16,3584]{2,1,0:T(8,128)(2,1)} %bitcast.38), calls=%async_computation | async-start | bytes 7340032 | tf_op jit(solution)/shard_map/all_to_all | solution.py:36
  16.8 3.1 copy-start.8
  19.3 3.9 collective-permute-start.1
  22.1 76.0 %collective-permute-start = (bf16[3584,256]{1,0:T(8,128)(2,1)}, bf16[3584,256]{1,0:T(8,128)(2,1)}, u32[]{:S(2)}, u32[]{:S(2)}) collective-permute-start(bf16[3584,256]{1,0:T(8,128)(2,1)} %get-tuple-element.48), channel_id=1, source_target_pairs={{0,1},{1,0},{2,3},{3,2},{4,5},{5,4},{6,7},{7,6},{8,9},{9,8},{10,11... | collective-permute-start | bytes 5505032 | tf_op jit(solution)/shard_map/ppermute | solution.py:32
  23.4 1.2 copy-start.1
  98.0 9.0 %copy-start.2 = (bf16[256,3584]{1,0:T(8,128)(2,1)S(1)}, bf16[256,3584]{1,0:T(8,128)(2,1)}, u32[]{:S(2)}) copy-start(bf16[256,3584]{1,0:T(8,128)(2,1)} %copy-done.1) | copy-start | bytes 5505028
  102.0 5.0 %collective-permute-start.2 = (f32[512,512]{1,0:T(8,128)S(1)}, f32[512,512]{1,0:T(8,128)S(1)}, u32[]{:S(2)}, u32[]{:S(2)}) collective-permute-start(f32[512,512]{1,0:T(8,128)S(1)} %shard_map.88.mine), channel_id=1, source_target_pairs={{0,1},{1,0},{2,3},{3,2},{4,5},{5,4},{6,7},{7,6},{8,9},{9,8},{10,11... | collective-permute-start | bytes 3145736 | tf_op jit(solution)/shard_map/ppermute | solution.py:32
  109.1 74.1 %copy-start.3 = (bf16[1,64,7168]{2,1,0:T(8,128)(2,1)S(1)}, bf16[1,64,7168]{2,1,0:T(8,128)(2,1)}, u32[]{:S(2)}) copy-start(bf16[1,64,7168]{2,1,0:T(8,128)(2,1)} %param.7) | copy-start | bytes 2752516
  109.1 74.1 %copy-start.4 = (bf16[1,64,7168]{2,1,0:T(8,128)(2,1)S(1)}, bf16[1,64,7168]{2,1,0:T(8,128)(2,1)}, u32[]{:S(2)}) copy-start(bf16[1,64,7168]{2,1,0:T(8,128)(2,1)} %param.8) | copy-start | bytes 2752516
  109.1 74.0 %copy-start.6 = (s32[1,2,2,64,1]{3,4,2,1,0:T(1,128)S(1)}, s32[1,2,2,64,1]{3,4,2,1,0:T(1,128)}, u32[]{:S(2)}) copy-start(s32[1,2,2,64,1]{3,4,2,1,0:T(1,128)} %param.10) | copy-start | bytes 3076
  109.2 74.0 %copy-start.7 = (f32[1,2,2,64,1]{3,4,2,1,0:T(1,128)S(1)}, f32[1,2,2,64,1]{3,4,2,1,0:T(1,128)}, u32[]{:S(2)}) copy-start(f32[1,2,2,64,1]{3,4,2,1,0:T(1,128)} %param.11) | copy-start | bytes 3076
  183.2 21.0 %copy-start = (bf16[3584,256]{1,0:T(8,128)(2,1)S(1)}, bf16[3584,256]{1,0:T(8,128)(2,1)}, u32[]{:S(2)}) copy-start(bf16[3584,256]{1,0:T(8,128)(2,1)} %get-tuple-element.33.kept.refs_0_) | copy-start | bytes 5505028
  185.0 42.8 %copy-start.5 = (f32[1,7168]{1,0:T(1,128)S(1)}, f32[1,7168]{1,0:T(1,128)}, u32[]{:S(2)}) copy-start(f32[1,7168]{1,0:T(1,128)} %gain.3) | copy-start | bytes 86020
  185.0 38.8 %collective-permute-start.3 = (bf16[64,7168]{1,0:T(8,128)(2,1)S(1)}, bf16[64,7168]{1,0:T(8,128)(2,1)S(1)}, u32[]{:S(2)}, u32[]{:S(2)}) collective-permute-start(bf16[64,7168]{1,0:T(8,128)(2,1)S(1)} %get-tuple-element.31), channel_id=1, source_target_pairs={{0,32},{32,64},{64,96},{96,128},{128,160},{160,192},{192,224},{224... | collective-permute-start | bytes 2752520 | tf_op jit(solution)/shard_map/ppermute | solution.py:27
  204.2 23.6 %collective-permute-start.4 = (bf16[64,7168]{1,0:T(8,128)(2,1)S(1)}, bf16[64,7168]{1,0:T(8,128)(2,1)S(1)}, u32[]{:S(2)}, u32[]{:S(2)}) collective-permute-start(bf16[64,7168]{1,0:T(8,128)(2,1)S(1)} %get-tuple-element.32), channel_id=1, source_target_pairs={{0,224},{32,0},{64,32},{96,64},{128,96},{160,128},{192,160},{224,1... | collective-permute-start | bytes 2752520 | tf_op jit(solution)/shard_map/ppermute | solution.py:27
  321.6 3.2 collective-permute-start.5

commit v5 on v4

--- a/solution.py
+++ b/solution.py
@@ -171,81 +171,86 @@
             out[:, hidden:] += other
 
 
-def up_body(rows, kept, got, out):
+def up_body(low, rows, kept, got, out):
     hidden = kept.shape[1]
-    out[:, :hidden] = jnp.dot(rows[...], kept[...], preferred_element_type=F32)
-    out[:, hidden:] = jnp.dot(rows[...], got[...], preferred_element_type=F32)
-
-
-def up(rows, kept, got, streamed):
+    piece = rows[low : low + out.shape[0]]
+    out[:, :hidden] = jnp.dot(piece, kept[...], preferred_element_type=F32)
+    out[:, hidden:] = jnp.dot(piece, got[...], preferred_element_type=F32)
+
+
+def streamed_up(rows, kept, got):
     count, part = rows.shape
-    scratch = [
-        pltpu.VMEM(rows.shape, BF16),
-        pltpu.VMEM(kept.shape, BF16),
-        pltpu.VMEM(got.shape, BF16),
-        pltpu.SemaphoreType.DMA((3 * len(tiles(part)),)),
-    ]
-    return pl.pallas_call(
-        streamed_up_body if streamed else up_body,
+    return pl.pallas_call(
+        streamed_up_body,
         out_shape=pltpu.VMEM((count, CORES * kept.shape[1]), F32),
-        in_specs=[pl.BlockSpec(memory_space=pl.ANY if streamed else pltpu.VMEM)] * 3,
+        in_specs=[pl.BlockSpec(memory_space=pl.ANY)] * 3,
         out_specs=pl.BlockSpec(memory_space=pltpu.VMEM),
-        scratch_shapes=scratch if streamed else [],
-        compiler_params=params(LARGE if streamed else SMALL),
+        scratch_shapes=[
+            pltpu.VMEM(rows.shape, BF16),
+            pltpu.VMEM(kept.shape, BF16),
+            pltpu.VMEM(got.shape, BF16),
+            pltpu.SemaphoreType.DMA((3 * len(tiles(part)),)),
+        ],
+        compiler_params=params(LARGE),
     )(rows, kept, got)
 
 
-def down_body(mine, theirs, kept, got, out):
-    hidden = kept.shape[0]
-    first = jax.nn.silu(mine[:, :hidden] + theirs[:, hidden:]).astype(BF16)
-    second = jax.nn.silu(mine[:, hidden:] + theirs[:, :hidden]).astype(BF16)
-    for low, high in tiles(kept.shape[1]):
-        total = jnp.dot(first, kept[:, low:high], preferred_element_type=F32)
-        total = total + jnp.dot(second, got[:, low:high], preferred_element_type=F32)
-        out[:, low:high] = total.astype(out.dtype)
-
-
-def down(mine, theirs, kept, got):
-    return pl.pallas_call(
-        down_body,
-        out_shape=jax.ShapeDtypeStruct((mine.shape[0], kept.shape[1]), BF16),
-        in_specs=[pl.BlockSpec(memory_space=pltpu.VMEM)] * 4,
+def up(rows, kept, got, low, count):
+    return pl.pallas_call(
+        functools.partial(up_body, low),
+        out_shape=pltpu.VMEM((count, CORES * kept.shape[1]), F32),
+        in_specs=[pl.BlockSpec(memory_space=pltpu.VMEM)] * 3,
         out_specs=pl.BlockSpec(memory_space=pltpu.VMEM),
         compiler_params=params(SMALL),
-    )(mine, theirs, kept, got)
-
-
-def finish_body(
-    capacity, moment, first, second, returned, routes, gates, new_first, new_second, held, sems
-):
+    )(rows, kept, got)
+
+
+def down_body(*refs):
+    sums, (kept, got, out) = refs[:-3], refs[-3:]
+    hidden = kept.shape[0]
+    active = []
+    for mine, theirs in zip(sums[0::2], sums[1::2]):
+        first = jax.nn.silu(mine[:, :hidden] + theirs[:, hidden:]).astype(BF16)
+        second = jax.nn.silu(mine[:, hidden:] + theirs[:, :hidden]).astype(BF16)
+        active.append((first, second))
+    for low, high in tiles(kept.shape[1]):
+        for i, (first, second) in enumerate(active):
+            rows = slice(i * first.shape[0], (i + 1) * first.shape[0])
+            total = jnp.dot(first, kept[:, low:high], preferred_element_type=F32)
+            total = total + jnp.dot(second, got[:, low:high], preferred_element_type=F32)
+            out[rows, low:high] = total.astype(out.dtype)
+
+
+def down(sums, kept, got):
+    count = sum(x.shape[0] for x in sums[0::2])
+    return pl.pallas_call(
+        down_body,
+        out_shape=jax.ShapeDtypeStruct((count, kept.shape[1]), BF16),
+        in_specs=[pl.BlockSpec(memory_space=pltpu.VMEM)] * (len(sums) + 2),
+        out_specs=pl.BlockSpec(memory_space=pltpu.VMEM),
+        compiler_params=params(SMALL),
+    )(*sums, kept, got)
+
+
+def finish_body(capacity, moment, first, second, returned, routes, gates, *refs):
+    outs, rest = refs[:COURSES], refs[COURSES:]
+    news = rest[:COURSES] if rest else outs
     experts = returned.shape[0]
     part = returned.shape[-1]
-    step = part // 2
-    spans = [(core, low) for core in range(CORES) for low in (0, step)]
-    copies = started(
-        [
-            (
-                returned.at[:, :, core, :, low : low + step],
-                held.at[:, :, core, :, low : low + step],
-            )
-            for core, low in spans
-        ],
-        sems,
-    )
     chosen = [column(routes[course, moment]) for course in range(COURSES)]
     tables = [tokens_by_slots(route, experts, capacity) for route in chosen]
     scales = [column(gates[course, moment]) for course in range(COURSES)]
-    for copy, (core, start) in zip(copies, spans):
-        copy.wait()
-        for low in range(start, start + step, TILE // 2):
+    leaving = []
+    for core in range(CORES):
+        for low in range(0, part, TILE // 2):
             high = low + TILE // 2
             summed = [
-                held[e, 0, core, :, low:high].astype(F32)
-                + held[e, 1, core, :, low:high].astype(F32)
+                returned[e, 0, core, :, low:high].astype(F32)
+                + returned[e, 1, core, :, low:high].astype(F32)
                 for e in range(experts)
             ]
             columns = slice(core * part + low, core * part + high)
-            for course, (state, new) in enumerate(((first, new_first), (second, new_second))):
+            for course, (state, new) in enumerate(((first, news[0]), (second, news[1]))):
                 span = slice(course * capacity, (course + 1) * capacity)
                 produced = jnp.concatenate([block[span] for block in summed], axis=0)
                 gathered = jnp.dot(
@@ -254,19 +259,33 @@
                 new[:, columns] = (
                     state[:, columns].astype(F32) + gathered * scales[course]
                 ).astype(BF16)
-
-
-def finish(states, returned, routes, gates, experts, capacity, moment):
+        if rest:
+            span = slice(core * part, (core + 1) * part)
+            for course in range(COURSES):
+                copy = pltpu.make_async_copy(
+                    news[course].at[:, span],
+                    outs[course].at[:, span],
+                    rest[COURSES].at[core, course],
+                )
+                copy.start()
+                leaving.append(copy)
+    for copy in leaving:
+        copy.wait()
+
+
+def finish(states, returned, routes, gates, experts, capacity, moment, last):
     tokens, width = states[0].shape
     rows, part = returned.shape[-2:]
     shape = (experts, HALVES, CORES, rows, part)
     vmem = pl.BlockSpec(memory_space=pltpu.VMEM)
+    scratch = [pltpu.VMEM((tokens, width), BF16)] * COURSES
+    scratch.append(pltpu.SemaphoreType.DMA((CORES, COURSES)))
     return pl.pallas_call(
         functools.partial(finish_body, capacity, moment),
         out_shape=[jax.ShapeDtypeStruct((tokens, width), BF16)] * COURSES,
-        in_specs=[vmem, vmem, pl.BlockSpec(memory_space=pl.ANY), vmem, vmem],
-        out_specs=[vmem] * COURSES,
-        scratch_shapes=[pltpu.VMEM(shape, BF16), pltpu.SemaphoreType.DMA((2 * CORES,))],
+        in_specs=[vmem] * 5,
+        out_specs=[pl.BlockSpec(memory_space=pl.ANY) if last else vmem] * COURSES,
+        scratch_shapes=scratch if last else [],
         compiler_params=params(SMALL),
     )(*states, returned.reshape(shape), routes, gates)
 
@@ -297,11 +316,16 @@
         sending = prepare(states, norm_gain, routes, experts, capacity, t, limit)
         rows = exchange(sending.reshape(block)).reshape(-1, part)
         rows, near_down = lax.optimization_barrier((rows, near_down))
-        sums = up(rows, up_kept, up_got, True) if t == 0 else up(rows, *near_up, False)
-        partial = down(sums, across_cores(sums), *near_down)
+        if t == 0:
+            sums = [streamed_up(rows, up_kept, up_got)]
+        else:
+            half = rows.shape[0] // 2
+            sums = [up(rows, *near_up, low, half) for low in (0, half)]
+        partial = down([x for mine in sums for x in (mine, across_cores(mine))], *near_down)
         returned = exchange(partial.reshape(block))
-        states = finish(states, returned, routes, gates, experts, capacity, t)
-        if t + 1 < STEPS:
+        last = t + 1 == STEPS
+        states = finish(states, returned, routes, gates, experts, capacity, t, last)
+        if not last:
             up_kept, up_got, *states = lax.optimization_barrier((up_kept, up_got, *states))
             near_up = hold(up_kept, up_got)
             states = [passed_along(states[c], "section", 1 - 2 * c) for c in range(COURSES)]

time: 420 us -> 419 us (level)
    pallas_call x4 -> x5, Pallas kernels: 10.2 us -> 10.4 us  [the longest x2 4.23 us: down(): pl.pallas_call(down_body, out_shape=jax.ShapeDtypeStruct((count, kept.sha...]
  transfers between devices with their start and end apart: 7 -> 8, of which waited for: 6 -> 7; matrix products, arithmetic and copies ran while one was open for 1% -> 1% of each run, Pallas kernels for 0% -> 0%
where the time goes in v5:
time: 419 us
  blocking collectives  254 us (61%)
  waiting for transfers between devices  101 us (24%)
  starting transfers between devices  35.9 us (9%)
  Pallas kernels  21.7 us (5%)
  local copies, waits for them, and re-layouts  6.09 us (1%)
    all_to_all x3, blocking collectives, exchange(): lax.all_to_all(blocks, 'expert', split_axis=0, concat_axis=0, tiled=True)  254 us
    all_to_all x1, waiting for transfers between devices, exchange(): lax.all_to_all(blocks, 'expert', split_axis=0, concat_axis=0, tiled=True)  73.4 us
    ppermute x2, waiting for transfers between devices, passed_along(): lax.ppermute(array, axis, [(i, (i + by) % size) for i in range(size)])  21.9 us
    ppermute x2, starting transfers between devices, passed_along(): lax.ppermute(array, axis, [(i, (i + by) % size) for i in range(size)])  19.2 us
    all_to_all x1, starting transfers between devices, exchange(): lax.all_to_all(blocks, 'expert', split_axis=0, concat_axis=0, tiled=True)  12 us
  transfers between devices with their start and end apart: 8, of which 7 were waited for; matrix products, arithmetic and copies ran while one was open for 1% of the time, Pallas kernels for 0%

profile of v5, /device:TPU:7, one launch (start us, length us, event | category | flops | bytes accessed | tf_op | source)
XLA Modules:
  0.0 418.9 jit_solution(12630531254378550817)
XLA Ops:
  0.6 4.1 shard_map.86
  4.8 12.0 %all-to-all-start = ((bf16[32,16,3584]{2,1,0:T(8,128)(2,1)}), bf16[32,16,3584]{2,1,0:T(8,128)(2,1)}, u32[]{:S(2)}, u32[]{:S(2)}) async-start(bf16[32,16,3584]{2,1,0:T(8,128)(2,1)} %bitcast.39), calls=%async_computation | async-start | bytes 7340032 | tf_op jit(solution)/shard_map/all_to_all | solution.py:36
  16.8 0.0 copy-start.8
  16.8 2.4 dynamic-slice_bitcast_fusion
  19.2 0.4 collective-permute-start.1
  19.6 0.3 copy-done.8
  19.9 2.1 dynamic-slice_bitcast_fusion.2
  22.0 0.3 collective-permute-start
  22.3 0.8 collective-permute-done.1.refs_1_
  23.1 0.3 shard_map.87
  23.4 0.0 copy-start.1
  23.4 1.2 copy-done.1
  24.6 73.4 %all-to-all-done = bf16[32,16,3584]{2,1,0:T(8,128)(2,1)} async-done(((bf16[32,16,3584]{2,1,0:T(8,128)(2,1)}), bf16[32,16,3584]{2,1,0:T(8,128)(2,1)}, u32[]{:S(2)}, u32[]{:S(2)}) %all-to-all-start) | async-done | bytes 3670048 | tf_op jit(solution)/shard_map/all_to_all | solution.py:36
  98.0 0.0 collective-permute-done.got.refs_1_
  98.0 0.0 copy-start.2
  98.0 3.9 shard_map.88.refs_0_
  101.9 2.7 collective-permute-start.2
  104.7 2.3 collective-permute-done.2.refs_1_
  107.0 0.0 copy-done.2
  107.0 2.1 shard_map.89
  109.1 0.0 copy-start.3
  109.1 0.0 copy-start.4
  109.1 0.0 copy-start.6
  109.1 0.0 copy-start.7
  109.1 74.0 %all_to_all.20 = bf16[32,16,3584]{2,1,0:T(8,128)(2,1)S(1)} all-to-all(bf16[32,16,3584]{2,1,0:T(8,128)(2,1)S(1)} %bitcast.25), channel_id=1, replica_groups=mesh['section'=8,'expert'=32] {'expert'}, dimensions={0} | all-to-all | bytes 7340032 | tf_op jit(solution)/shard_map/all_to_all | solution.py:36
  183.1 0.0 copy-done.3
  183.1 0.0 copy-done.4
  183.2 0.0 copy-done.6
  183.2 0.0 copy-done.7
  183.2 0.0 copy-start
  183.2 1.4 shard_map.90
  184.6 0.0 copy-start.5
  184.6 19.2 %collective-permute-start.3 = (bf16[64,7168]{1,0:T(8,128)(2,1)S(1)}, bf16[64,7168]{1,0:T(8,128)(2,1)S(1)}, u32[]{:S(2)}, u32[]{:S(2)}) collective-permute-start(bf16[64,7168]{1,0:T(8,128)(2,1)S(1)} %get-tuple-element.31), channel_id=1, source_target_pairs={{0,32},{32,64},{64,96},{96,128},{128,160},{160,192},{192,224},{224... | collective-permute-start | bytes 2752520 | tf_op jit(solution)/shard_map/ppermute | solution.py:27
  203.8 0.0 collective-permute-start.4
  203.8 0.0 copy-done
  203.8 1.6 shard_map.91
  205.4 17.9 %collective-permute-done.3.first = bf16[64,7168]{1,0:T(8,128)(2,1)S(1)} collective-permute-done((bf16[64,7168]{1,0:T(8,128)(2,1)S(1)}, bf16[64,7168]{1,0:T(8,128)(2,1)S(1)}, u32[]{:S(2)}, u32[]{:S(2)}) %collective-permute-start.3) | collective-permute-done | bytes 917536 | tf_op jit(solution)/shard_map/ppermute | solution.py:27
  223.4 4.0 collective-permute-done.4.second
  227.4 0.0 copy-done.5
  227.4 1.6 shard_map.92
  229.0 90.1 %all_to_all.21 = bf16[32,16,3584]{2,1,0:T(8,128)(2,1)S(1)} all-to-all(bf16[32,16,3584]{2,1,0:T(8,128)(2,1)S(1)} %bitcast.28), channel_id=1, replica_groups=mesh['section'=8,'expert'=32] {'expert'}, dimensions={0} | all-to-all | bytes 7340032 | tf_op jit(solution)/shard_map/all_to_all | solution.py:36
  319.0 1.1 shard_map.94.refs_2_
  320.1 1.1 shard_map.93.refs_0_
  321.3 1.2 collective-permute-start.5
  322.4 0.1 collective-permute-start.6
  322.5 1.4 collective-permute-done.5.refs_1_
  324.0 0.7 collective-permute-done.6.refs_3_
  324.7 2.1 shard_map.95
  326.9 89.6 %all_to_all.22 = bf16[32,16,3584]{2,1,0:T(8,128)(2,1)S(1)} all-to-all(bf16[32,16,3584]{2,1,0:T(8,128)(2,1)S(1)} %bitcast.24), channel_id=1, replica_groups=mesh['section'=8,'expert'=32] {'expert'}, dimensions={0} | all-to-all | bytes 7340032 | tf_op jit(solution)/shard_map/all_to_all | solution.py:36
  416.4 2.3 shard_map.96
Async XLA Ops:
  4.8 93.2 %all-to-all-start = ((bf16[32,16,3584]{2,1,0:T(8,128)(2,1)}), bf16[32,16,3584]{2,1,0:T(8,128)(2,1)}, u32[]{:S(2)}, u32[]{:S(2)}) async-start(bf16[32,16,3584]{2,1,0:T(8,128)(2,1)} %bitcast.39), calls=%async_computation | async-start | bytes 7340032 | tf_op jit(solution)/shard_map/all_to_all | solution.py:36
  16.8 3.1 copy-start.8
  19.2 3.9 collective-permute-start.1
  22.0 76.0 %collective-permute-start = (bf16[3584,256]{1,0:T(8,128)(2,1)}, bf16[3584,256]{1,0:T(8,128)(2,1)}, u32[]{:S(2)}, u32[]{:S(2)}) collective-permute-start(bf16[3584,256]{1,0:T(8,128)(2,1)} %get-tuple-element.48), channel_id=1, source_target_pairs={{0,1},{1,0},{2,3},{3,2},{4,5},{5,4},{6,7},{7,6},{8,9},{9,8},{10,11... | collective-permute-start | bytes 5505032 | tf_op jit(solution)/shard_map/ppermute | solution.py:32
  23.4 1.2 copy-start.1
  98.0 9.0 %copy-start.2 = (bf16[256,3584]{1,0:T(8,128)(2,1)S(1)}, bf16[256,3584]{1,0:T(8,128)(2,1)}, u32[]{:S(2)}) copy-start(bf16[256,3584]{1,0:T(8,128)(2,1)} %copy-done.1) | copy-start | bytes 5505028
  101.9 5.0 %collective-permute-start.2 = (f32[512,512]{1,0:T(8,128)S(1)}, f32[512,512]{1,0:T(8,128)S(1)}, u32[]{:S(2)}, u32[]{:S(2)}) collective-permute-start(f32[512,512]{1,0:T(8,128)S(1)} %shard_map.88.refs_0_), channel_id=1, source_target_pairs={{0,1},{1,0},{2,3},{3,2},{4,5},{5,4},{6,7},{7,6},{8,9},{9,8},{10,11... | collective-permute-start | bytes 3145736 | tf_op jit(solution)/shard_map/ppermute | solution.py:32
  109.1 74.1 %copy-start.3 = (bf16[1,64,7168]{2,1,0:T(8,128)(2,1)S(1)}, bf16[1,64,7168]{2,1,0:T(8,128)(2,1)}, u32[]{:S(2)}) copy-start(bf16[1,64,7168]{2,1,0:T(8,128)(2,1)} %param.7) | copy-start | bytes 2752516
  109.1 74.1 %copy-start.4 = (bf16[1,64,7168]{2,1,0:T(8,128)(2,1)S(1)}, bf16[1,64,7168]{2,1,0:T(8,128)(2,1)}, u32[]{:S(2)}) copy-start(bf16[1,64,7168]{2,1,0:T(8,128)(2,1)} %param.8) | copy-start | bytes 2752516
  109.1 74.0 %copy-start.6 = (s32[1,2,2,64,1]{3,4,2,1,0:T(1,128)S(1)}, s32[1,2,2,64,1]{3,4,2,1,0:T(1,128)}, u32[]{:S(2)}) copy-start(s32[1,2,2,64,1]{3,4,2,1,0:T(1,128)} %param.10) | copy-start | bytes 3076
  109.1 74.0 %copy-start.7 = (f32[1,2,2,64,1]{3,4,2,1,0:T(1,128)S(1)}, f32[1,2,2,64,1]{3,4,2,1,0:T(1,128)}, u32[]{:S(2)}) copy-start(f32[1,2,2,64,1]{3,4,2,1,0:T(1,128)} %param.11) | copy-start | bytes 3076
  183.2 20.6 %copy-start = (bf16[3584,256]{1,0:T(8,128)(2,1)S(1)}, bf16[3584,256]{1,0:T(8,128)(2,1)}, u32[]{:S(2)}) copy-start(bf16[3584,256]{1,0:T(8,128)(2,1)} %get-tuple-element.33.kept.refs_0_) | copy-start | bytes 5505028
  184.6 42.8 %copy-start.5 = (f32[1,7168]{1,0:T(1,128)S(1)}, f32[1,7168]{1,0:T(1,128)}, u32[]{:S(2)}) copy-start(f32[1,7168]{1,0:T(1,128)} %gain.3) | copy-start | bytes 86020
  184.6 38.8 %collective-permute-start.3 = (bf16[64,7168]{1,0:T(8,128)(2,1)S(1)}, bf16[64,7168]{1,0:T(8,128)(2,1)S(1)}, u32[]{:S(2)}, u32[]{:S(2)}) collective-permute-start(bf16[64,7168]{1,0:T(8,128)(2,1)S(1)} %get-tuple-element.31), channel_id=1, source_target_pairs={{0,32},{32,64},{64,96},{96,128},{128,160},{160,192},{192,224},{224... | collective-permute-start | bytes 2752520 | tf_op jit(solution)/shard_map/ppermute | solution.py:27
  203.8 23.6 %collective-permute-start.4 = (bf16[64,7168]{1,0:T(8,128)(2,1)S(1)}, bf16[64,7168]{1,0:T(8,128)(2,1)S(1)}, u32[]{:S(2)}, u32[]{:S(2)}) collective-permute-start(bf16[64,7168]{1,0:T(8,128)(2,1)S(1)} %get-tuple-element.32), channel_id=1, source_target_pairs={{0,224},{32,0},{64,32},{96,64},{128,96},{160,128},{192,160},{224,1... | collective-permute-start | bytes 2752520 | tf_op jit(solution)/shard_map/ppermute | solution.py:27
  321.3 2.7 collective-permute-start.5
  322.4 2.3 collective-permute-start.6

commit v6 on v5

--- a/solution.py
+++ b/solution.py
@@ -171,11 +171,10 @@
             out[:, hidden:] += other
 
 
-def up_body(low, rows, kept, got, out):
+def up_body(rows, kept, got, out):
     hidden = kept.shape[1]
-    piece = rows[low : low + out.shape[0]]
-    out[:, :hidden] = jnp.dot(piece, kept[...], preferred_element_type=F32)
-    out[:, hidden:] = jnp.dot(piece, got[...], preferred_element_type=F32)
+    out[:, :hidden] = jnp.dot(rows[...], kept[...], preferred_element_type=F32)
+    out[:, hidden:] = jnp.dot(rows[...], got[...], preferred_element_type=F32)
 
 
 def streamed_up(rows, kept, got):
@@ -195,10 +194,10 @@
     )(rows, kept, got)
 
 
-def up(rows, kept, got, low, count):
-    return pl.pallas_call(
-        functools.partial(up_body, low),
-        out_shape=pltpu.VMEM((count, CORES * kept.shape[1]), F32),
+def up(rows, kept, got):
+    return pl.pallas_call(
+        up_body,
+        out_shape=pltpu.VMEM((rows.shape[0], CORES * kept.shape[1]), F32),
         in_specs=[pl.BlockSpec(memory_space=pltpu.VMEM)] * 3,
         out_specs=pl.BlockSpec(memory_space=pltpu.VMEM),
         compiler_params=params(SMALL),
@@ -319,8 +318,7 @@
         if t == 0:
             sums = [streamed_up(rows, up_kept, up_got)]
         else:
-            half = rows.shape[0] // 2
-            sums = [up(rows, *near_up, low, half) for low in (0, half)]
+            sums = [up(rows, *near_up)]
         partial = down([x for mine in sums for x in (mine, across_cores(mine))], *near_down)
         returned = exchange(partial.reshape(block))
         last = t + 1 == STEPS

time: 419 us -> 419 us (level)
  transfers between devices with their start and end apart: 8 -> 7, of which waited for: 7 -> 6; matrix products, arithmetic and copies ran while one was open for 1% -> 1% of each run, Pallas kernels for 0% -> 0%
where the time goes in v6:
time: 419 us
  blocking collectives  254 us (61%)
  waiting for transfers between devices  101 us (24%)
  starting transfers between devices  35.7 us (9%)
  Pallas kernels  21.6 us (5%)
  local copies, waits for them, and re-layouts  6.09 us (1%)
    all_to_all x3, blocking collectives, exchange(): lax.all_to_all(blocks, 'expert', split_axis=0, concat_axis=0, tiled=True)  254 us
    all_to_all x1, waiting for transfers between devices, exchange(): lax.all_to_all(blocks, 'expert', split_axis=0, concat_axis=0, tiled=True)  73.4 us
    ppermute x2, waiting for transfers between devices, passed_along(): lax.ppermute(array, axis, [(i, (i + by) % size) for i in range(size)])  21.9 us
    ppermute x2, starting transfers between devices, passed_along(): lax.ppermute(array, axis, [(i, (i + by) % size) for i in range(size)])  19.2 us
    all_to_all x1, starting transfers between devices, exchange(): lax.all_to_all(blocks, 'expert', split_axis=0, concat_axis=0, tiled=True)  12 us
  transfers between devices with their start and end apart: 7, of which 6 were waited for; matrix products, arithmetic and copies ran while one was open for 1% of the time, Pallas kernels for 0%

profile of v6, /device:TPU:7, one launch (start us, length us, event | category | flops | bytes accessed | tf_op | source)
XLA Modules:
  0.0 418.7 jit_solution(12476450405360556448)
XLA Ops:
  0.6 4.2 shard_map.86
  4.8 12.0 %all-to-all-start = ((bf16[32,16,3584]{2,1,0:T(8,128)(2,1)}), bf16[32,16,3584]{2,1,0:T(8,128)(2,1)}, u32[]{:S(2)}, u32[]{:S(2)}) async-start(bf16[32,16,3584]{2,1,0:T(8,128)(2,1)} %bitcast.38), calls=%async_computation | async-start | bytes 7340032 | tf_op jit(solution)/shard_map/all_to_all | solution.py:36
  16.8 0.0 copy-start.8
  16.8 2.4 dynamic-slice_bitcast_fusion
  19.3 0.4 collective-permute-start.1
  19.7 0.3 copy-done.8
  20.0 2.1 dynamic-slice_bitcast_fusion.2
  22.1 0.3 collective-permute-start
  22.4 0.8 collective-permute-done.1.refs_1_
  23.1 0.3 shard_map.87
  23.4 0.0 copy-start.1
  23.4 1.2 copy-done.1
  24.6 73.4 %all-to-all-done = bf16[32,16,3584]{2,1,0:T(8,128)(2,1)} async-done(((bf16[32,16,3584]{2,1,0:T(8,128)(2,1)}), bf16[32,16,3584]{2,1,0:T(8,128)(2,1)}, u32[]{:S(2)}, u32[]{:S(2)}) %all-to-all-start) | async-done | bytes 3670048 | tf_op jit(solution)/shard_map/all_to_all | solution.py:36
  98.0 0.0 collective-permute-done.got.refs_1_
  98.0 0.0 copy-start.2
  98.1 3.9 shard_map.88.refs_0_
  102.0 2.7 collective-permute-start.2
  104.7 2.3 collective-permute-done.2.refs_1_
  107.0 0.0 copy-done.2
  107.0 2.1 shard_map.89
  109.1 0.0 copy-start.3
  109.1 0.0 copy-start.4
  109.1 0.0 copy-start.6
  109.2 0.0 copy-start.7
  109.2 74.0 %all_to_all.20 = bf16[32,16,3584]{2,1,0:T(8,128)(2,1)S(1)} all-to-all(bf16[32,16,3584]{2,1,0:T(8,128)(2,1)S(1)} %bitcast.23), channel_id=1, replica_groups=mesh['section'=8,'expert'=32] {'expert'}, dimensions={0} | all-to-all | bytes 7340032 | tf_op jit(solution)/shard_map/all_to_all | solution.py:36
  183.2 0.0 copy-done.3
  183.2 0.0 copy-done.4
  183.2 0.0 copy-done.6
  183.2 0.0 copy-done.7
  183.2 0.0 copy-start
  183.2 1.4 shard_map.90
  184.6 0.0 copy-start.5
  184.6 19.2 %collective-permute-start.3 = (bf16[64,7168]{1,0:T(8,128)(2,1)S(1)}, bf16[64,7168]{1,0:T(8,128)(2,1)S(1)}, u32[]{:S(2)}, u32[]{:S(2)}) collective-permute-start(bf16[64,7168]{1,0:T(8,128)(2,1)S(1)} %get-tuple-element.31), channel_id=1, source_target_pairs={{0,32},{32,64},{64,96},{96,128},{128,160},{160,192},{192,224},{224... | collective-permute-start | bytes 2752520 | tf_op jit(solution)/shard_map/ppermute | solution.py:27
  203.8 0.0 collective-permute-start.4
  203.8 0.0 copy-done
  203.8 1.6 shard_map.91
  205.5 17.9 %collective-permute-done.3.first = bf16[64,7168]{1,0:T(8,128)(2,1)S(1)} collective-permute-done((bf16[64,7168]{1,0:T(8,128)(2,1)S(1)}, bf16[64,7168]{1,0:T(8,128)(2,1)S(1)}, u32[]{:S(2)}, u32[]{:S(2)}) %collective-permute-start.3) | collective-permute-done | bytes 917536 | tf_op jit(solution)/shard_map/ppermute | solution.py:27
  223.4 4.0 collective-permute-done.4.second
  227.4 0.0 copy-done.5
  227.4 1.6 shard_map.92
  229.0 90.2 %all_to_all.21 = bf16[32,16,3584]{2,1,0:T(8,128)(2,1)S(1)} all-to-all(bf16[32,16,3584]{2,1,0:T(8,128)(2,1)S(1)} %bitcast.27), channel_id=1, replica_groups=mesh['section'=8,'expert'=32] {'expert'}, dimensions={0} | all-to-all | bytes 7340032 | tf_op jit(solution)/shard_map/all_to_all | solution.py:36
  319.2 2.1 shard_map.93.refs_0_
  321.2 1.1 collective-permute-start.5
  322.3 2.3 collective-permute-done.5.refs_1_
  324.6 2.1 shard_map.94
  326.7 89.5 %all_to_all.22 = bf16[32,16,3584]{2,1,0:T(8,128)(2,1)S(1)} all-to-all(bf16[32,16,3584]{2,1,0:T(8,128)(2,1)S(1)} %bitcast.22), channel_id=1, replica_groups=mesh['section'=8,'expert'=32] {'expert'}, dimensions={0} | all-to-all | bytes 7340032 | tf_op jit(solution)/shard_map/all_to_all | solution.py:36
  416.2 2.3 shard_map.95
Async XLA Ops:
  4.8 93.2 %all-to-all-start = ((bf16[32,16,3584]{2,1,0:T(8,128)(2,1)}), bf16[32,16,3584]{2,1,0:T(8,128)(2,1)}, u32[]{:S(2)}, u32[]{:S(2)}) async-start(bf16[32,16,3584]{2,1,0:T(8,128)(2,1)} %bitcast.38), calls=%async_computation | async-start | bytes 7340032 | tf_op jit(solution)/shard_map/all_to_all | solution.py:36
  16.8 3.1 copy-start.8
  19.3 3.9 collective-permute-start.1
  22.1 76.0 %collective-permute-start = (bf16[3584,256]{1,0:T(8,128)(2,1)}, bf16[3584,256]{1,0:T(8,128)(2,1)}, u32[]{:S(2)}, u32[]{:S(2)}) collective-permute-start(bf16[3584,256]{1,0:T(8,128)(2,1)} %get-tuple-element.48), channel_id=1, source_target_pairs={{0,1},{1,0},{2,3},{3,2},{4,5},{5,4},{6,7},{7,6},{8,9},{9,8},{10,11... | collective-permute-start | bytes 5505032 | tf_op jit(solution)/shard_map/ppermute | solution.py:32
  23.4 1.2 copy-start.1
  98.0 9.0 %copy-start.2 = (bf16[256,3584]{1,0:T(8,128)(2,1)S(1)}, bf16[256,3584]{1,0:T(8,128)(2,1)}, u32[]{:S(2)}) copy-start(bf16[256,3584]{1,0:T(8,128)(2,1)} %copy-done.1) | copy-start | bytes 5505028
  102.0 5.0 %collective-permute-start.2 = (f32[512,512]{1,0:T(8,128)S(1)}, f32[512,512]{1,0:T(8,128)S(1)}, u32[]{:S(2)}, u32[]{:S(2)}) collective-permute-start(f32[512,512]{1,0:T(8,128)S(1)} %shard_map.88.refs_0_), channel_id=1, source_target_pairs={{0,1},{1,0},{2,3},{3,2},{4,5},{5,4},{6,7},{7,6},{8,9},{9,8},{10,11... | collective-permute-start | bytes 3145736 | tf_op jit(solution)/shard_map/ppermute | solution.py:32
  109.1 74.1 %copy-start.3 = (bf16[1,64,7168]{2,1,0:T(8,128)(2,1)S(1)}, bf16[1,64,7168]{2,1,0:T(8,128)(2,1)}, u32[]{:S(2)}) copy-start(bf16[1,64,7168]{2,1,0:T(8,128)(2,1)} %param.7) | copy-start | bytes 2752516
  109.1 74.1 %copy-start.4 = (bf16[1,64,7168]{2,1,0:T(8,128)(2,1)S(1)}, bf16[1,64,7168]{2,1,0:T(8,128)(2,1)}, u32[]{:S(2)}) copy-start(bf16[1,64,7168]{2,1,0:T(8,128)(2,1)} %param.8) | copy-start | bytes 2752516
  109.1 74.0 %copy-start.6 = (s32[1,2,2,64,1]{3,4,2,1,0:T(1,128)S(1)}, s32[1,2,2,64,1]{3,4,2,1,0:T(1,128)}, u32[]{:S(2)}) copy-start(s32[1,2,2,64,1]{3,4,2,1,0:T(1,128)} %param.10) | copy-start | bytes 3076
  109.2 74.0 %copy-start.7 = (f32[1,2,2,64,1]{3,4,2,1,0:T(1,128)S(1)}, f32[1,2,2,64,1]{3,4,2,1,0:T(1,128)}, u32[]{:S(2)}) copy-start(f32[1,2,2,64,1]{3,4,2,1,0:T(1,128)} %param.11) | copy-start | bytes 3076
  183.2 20.6 %copy-start = (bf16[3584,256]{1,0:T(8,128)(2,1)S(1)}, bf16[3584,256]{1,0:T(8,128)(2,1)}, u32[]{:S(2)}) copy-start(bf16[3584,256]{1,0:T(8,128)(2,1)} %get-tuple-element.33.kept.refs_0_) | copy-start | bytes 5505028
  184.6 42.8 %copy-start.5 = (f32[1,7168]{1,0:T(1,128)S(1)}, f32[1,7168]{1,0:T(1,128)}, u32[]{:S(2)}) copy-start(f32[1,7168]{1,0:T(1,128)} %gain.3) | copy-start | bytes 86020
  184.6 38.8 %collective-permute-start.3 = (bf16[64,7168]{1,0:T(8,128)(2,1)S(1)}, bf16[64,7168]{1,0:T(8,128)(2,1)S(1)}, u32[]{:S(2)}, u32[]{:S(2)}) collective-permute-start(bf16[64,7168]{1,0:T(8,128)(2,1)S(1)} %get-tuple-element.31), channel_id=1, source_target_pairs={{0,32},{32,64},{64,96},{96,128},{128,160},{160,192},{192,224},{224... | collective-permute-start | bytes 2752520 | tf_op jit(solution)/shard_map/ppermute | solution.py:27
  203.8 23.6 %collective-permute-start.4 = (bf16[64,7168]{1,0:T(8,128)(2,1)S(1)}, bf16[64,7168]{1,0:T(8,128)(2,1)S(1)}, u32[]{:S(2)}, u32[]{:S(2)}) collective-permute-start(bf16[64,7168]{1,0:T(8,128)(2,1)S(1)} %get-tuple-element.32), channel_id=1, source_target_pairs={{0,224},{32,0},{64,32},{96,64},{128,96},{160,128},{192,160},{224,1... | collective-permute-start | bytes 2752520 | tf_op jit(solution)/shard_map/ppermute | solution.py:27
  321.2 3.4 collective-permute-start.5

commit v7 on v6

--- a/solution.py
+++ b/solution.py
@@ -147,6 +147,23 @@
     )(*arrays)
 
 
+def stack_body(first, second, out, sems):
+    rows = first.shape[0]
+    for copy in started([(first, out.at[:rows]), (second, out.at[rows:])], sems):
+        copy.wait()
+
+
+def stack(first, second):
+    return pl.pallas_call(
+        stack_body,
+        out_shape=pltpu.VMEM((2 * first.shape[0], first.shape[1]), first.dtype),
+        in_specs=[pl.BlockSpec(memory_space=pl.ANY)] * 2,
+        out_specs=pl.BlockSpec(memory_space=pltpu.VMEM),
+        scratch_shapes=[pltpu.SemaphoreType.DMA((2,))],
+        compiler_params=params(SMALL),
+    )(first, second)
+
+
 def streamed_up_body(rows, kept, got, out, rows_held, kept_held, got_held, sems):
     hidden = kept.shape[1]
     bounds = tiles(rows.shape[1])
@@ -204,31 +221,24 @@
     )(rows, kept, got)
 
 
-def down_body(*refs):
-    sums, (kept, got, out) = refs[:-3], refs[-3:]
-    hidden = kept.shape[0]
-    active = []
-    for mine, theirs in zip(sums[0::2], sums[1::2]):
-        first = jax.nn.silu(mine[:, :hidden] + theirs[:, hidden:]).astype(BF16)
-        second = jax.nn.silu(mine[:, hidden:] + theirs[:, :hidden]).astype(BF16)
-        active.append((first, second))
-    for low, high in tiles(kept.shape[1]):
-        for i, (first, second) in enumerate(active):
-            rows = slice(i * first.shape[0], (i + 1) * first.shape[0])
-            total = jnp.dot(first, kept[:, low:high], preferred_element_type=F32)
-            total = total + jnp.dot(second, got[:, low:high], preferred_element_type=F32)
-            out[rows, low:high] = total.astype(out.dtype)
-
-
-def down(sums, kept, got):
-    count = sum(x.shape[0] for x in sums[0::2])
+def down_body(mine, theirs, weight, out):
+    hidden = weight.shape[0] // CORES
+    first = jax.nn.silu(mine[:, :hidden] + theirs[:, hidden:]).astype(BF16)
+    second = jax.nn.silu(mine[:, hidden:] + theirs[:, :hidden]).astype(BF16)
+    active = jnp.concatenate([first, second], axis=1)
+    for low, high in tiles(weight.shape[1]):
+        total = jnp.dot(active, weight[:, low:high], preferred_element_type=F32)
+        out[:, low:high] = total.astype(out.dtype)
+
+
+def down(mine, theirs, weight):
     return pl.pallas_call(
         down_body,
-        out_shape=jax.ShapeDtypeStruct((count, kept.shape[1]), BF16),
-        in_specs=[pl.BlockSpec(memory_space=pltpu.VMEM)] * (len(sums) + 2),
+        out_shape=jax.ShapeDtypeStruct((mine.shape[0], weight.shape[1]), BF16),
+        in_specs=[pl.BlockSpec(memory_space=pltpu.VMEM)] * 3,
         out_specs=pl.BlockSpec(memory_space=pltpu.VMEM),
         compiler_params=params(SMALL),
-    )(*sums, kept, got)
+    )(mine, theirs, weight)
 
 
 def finish_body(capacity, moment, first, second, returned, routes, gates, *refs):
@@ -307,7 +317,7 @@
     up_kept = lax.dynamic_slice_in_dim(up_own, core * part, part, 0)
     down_kept = lax.dynamic_slice_in_dim(down_own, core * part, part, 1)
 
-    near_down = hold(down_kept, down_got)
+    near_down = stack(down_kept, down_got)
     lines = (COURSES, STEPS, 1, tokens)
     routes, gates = routes.reshape(lines), gate_values.reshape(lines)
     for t in range(STEPS):
@@ -316,10 +326,10 @@
         rows = exchange(sending.reshape(block)).reshape(-1, part)
         rows, near_down = lax.optimization_barrier((rows, near_down))
         if t == 0:
-            sums = [streamed_up(rows, up_kept, up_got)]
+            sums = streamed_up(rows, up_kept, up_got)
         else:
-            sums = [up(rows, *near_up)]
-        partial = down([x for mine in sums for x in (mine, across_cores(mine))], *near_down)
+            sums = up(rows, *near_up)
+        partial = down(sums, across_cores(sums), near_down)
         returned = exchange(partial.reshape(block))
         last = t + 1 == STEPS
         states = finish(states, returned, routes, gates, experts, capacity, t, last)

time: 419 us -> 420 us (level)
  no operation moved by 1% of the time
where the time goes in v7:
time: 420 us
  blocking collectives  254 us (60%)
  waiting for transfers between devices  101 us (24%)
  starting transfers between devices  35.8 us (9%)
  Pallas kernels  20.2 us (5%)
  local copies, waits for them, and re-layouts  8.08 us (2%)
    all_to_all x3, blocking collectives, exchange(): lax.all_to_all(blocks, 'expert', split_axis=0, concat_axis=0, tiled=True)  254 us
    all_to_all x1, waiting for transfers between devices, exchange(): lax.all_to_all(blocks, 'expert', split_axis=0, concat_axis=0, tiled=True)  72.7 us
    ppermute x2, waiting for transfers between devices, passed_along(): lax.ppermute(array, axis, [(i, (i + by) % size) for i in range(size)])  23.3 us
    ppermute x2, starting transfers between devices, passed_along(): lax.ppermute(array, axis, [(i, (i + by) % size) for i in range(size)])  19.2 us
    all_to_all x1, starting transfers between devices, exchange(): lax.all_to_all(blocks, 'expert', split_axis=0, concat_axis=0, tiled=True)  12 us
  transfers between devices with their start and end apart: 7, of which 6 were waited for; matrix products, arithmetic and copies ran while one was open for 1% of the time, Pallas kernels for 0%

profile of v7, /device:TPU:7, one launch (start us, length us, event | category | flops | bytes accessed | tf_op | source)
XLA Modules:
  0.0 420.0 jit_solution(6671904981727596951)
XLA Ops:
  0.6 4.1 shard_map.86
  4.8 12.0 %all-to-all-start = ((bf16[32,16,3584]{2,1,0:T(8,128)(2,1)}), bf16[32,16,3584]{2,1,0:T(8,128)(2,1)}, u32[]{:S(2)}, u32[]{:S(2)}) async-start(bf16[32,16,3584]{2,1,0:T(8,128)(2,1)} %bitcast.38), calls=%async_computation | async-start | bytes 7340032 | tf_op jit(solution)/shard_map/all_to_all | solution.py:36
  16.8 0.0 copy-start.10
  16.8 2.4 dynamic-slice_bitcast_fusion
  19.2 0.4 collective-permute-start.1
  19.6 0.3 copy-done.10
  19.9 2.1 dynamic-slice_bitcast_fusion.2
  22.1 0.3 collective-permute-start
  22.4 0.8 collective-permute-done.1.second
  23.1 0.3 shard_map.87.weight
  23.4 0.0 copy-start
  23.4 1.9 copy-done
  25.3 72.7 %all-to-all-done = bf16[32,16,3584]{2,1,0:T(8,128)(2,1)} async-done(((bf16[32,16,3584]{2,1,0:T(8,128)(2,1)}), bf16[32,16,3584]{2,1,0:T(8,128)(2,1)}, u32[]{:S(2)}, u32[]{:S(2)}) %all-to-all-start) | async-done | bytes 3670048 | tf_op jit(solution)/shard_map/all_to_all | solution.py:36
  98.0 0.0 collective-permute-done.got.refs_1_
  98.0 0.0 copy-start.3
  98.0 1.2 copy-done.3
  99.3 0.0 copy-start.1
  99.3 3.9 shard_map.88.mine
  103.2 2.7 collective-permute-start.2
  106.0 2.3 collective-permute-done.2.theirs
  108.2 0.0 copy-done.1
  108.2 2.1 shard_map.89
  110.3 0.0 copy-start.5
  110.4 0.0 copy-start.6
  110.4 0.0 copy-start.8
  110.4 0.0 copy-start.9
  110.4 74.0 %all_to_all.20 = bf16[32,16,3584]{2,1,0:T(8,128)(2,1)S(1)} all-to-all(bf16[32,16,3584]{2,1,0:T(8,128)(2,1)S(1)} %bitcast.23), channel_id=1, replica_groups=mesh['section'=8,'expert'=32] {'expert'}, dimensions={0} | all-to-all | bytes 7340032 | tf_op jit(solution)/shard_map/all_to_all | solution.py:36
  184.4 0.0 copy-start.2
  184.4 0.0 copy-start.4
  184.4 0.0 copy-done.5
  184.4 0.0 copy-done.6
  184.4 0.0 copy-done.8
  184.4 0.0 copy-done.9
  184.5 0.0 copy-start.7
  184.5 1.4 shard_map.90
  185.9 19.2 %collective-permute-start.3 = (bf16[64,7168]{1,0:T(8,128)(2,1)S(1)}, bf16[64,7168]{1,0:T(8,128)(2,1)S(1)}, u32[]{:S(2)}, u32[]{:S(2)}) collective-permute-start(bf16[64,7168]{1,0:T(8,128)(2,1)S(1)} %get-tuple-element.24), channel_id=1, source_target_pairs={{0,32},{32,64},{64,96},{96,128},{128,160},{160,192},{192,224},{224... | collective-permute-start | bytes 2752520 | tf_op jit(solution)/shard_map/ppermute | solution.py:27
  205.1 0.0 collective-permute-start.4
  205.1 0.0 copy-done.2
  205.1 0.0 copy-done.4
  205.1 0.3 shard_map.91
  205.4 19.3 %collective-permute-done.3.first = bf16[64,7168]{1,0:T(8,128)(2,1)S(1)} collective-permute-done((bf16[64,7168]{1,0:T(8,128)(2,1)S(1)}, bf16[64,7168]{1,0:T(8,128)(2,1)S(1)}, u32[]{:S(2)}, u32[]{:S(2)}) %collective-permute-start.3) | collective-permute-done | bytes 917536 | tf_op jit(solution)/shard_map/ppermute | solution.py:27
  224.7 4.0 collective-permute-done.4.second
  228.7 0.0 copy-done.7
  228.7 1.6 shard_map.92
  230.3 90.0 %all_to_all.21 = bf16[32,16,3584]{2,1,0:T(8,128)(2,1)S(1)} all-to-all(bf16[32,16,3584]{2,1,0:T(8,128)(2,1)S(1)} %bitcast.27), channel_id=1, replica_groups=mesh['section'=8,'expert'=32] {'expert'}, dimensions={0} | all-to-all | bytes 7340032 | tf_op jit(solution)/shard_map/all_to_all | solution.py:36
  320.3 2.1 shard_map.93.mine
  322.4 1.2 collective-permute-start.5
  323.5 2.3 collective-permute-done.5.theirs
  325.8 2.1 shard_map.94
  327.9 89.6 %all_to_all.22 = bf16[32,16,3584]{2,1,0:T(8,128)(2,1)S(1)} all-to-all(bf16[32,16,3584]{2,1,0:T(8,128)(2,1)S(1)} %bitcast.22), channel_id=1, replica_groups=mesh['section'=8,'expert'=32] {'expert'}, dimensions={0} | all-to-all | bytes 7340032 | tf_op jit(solution)/shard_map/all_to_all | solution.py:36
  417.5 2.3 shard_map.95
Async XLA Ops:
  4.8 93.2 %all-to-all-start = ((bf16[32,16,3584]{2,1,0:T(8,128)(2,1)}), bf16[32,16,3584]{2,1,0:T(8,128)(2,1)}, u32[]{:S(2)}, u32[]{:S(2)}) async-start(bf16[32,16,3584]{2,1,0:T(8,128)(2,1)} %bitcast.38), calls=%async_computation | async-start | bytes 7340032 | tf_op jit(solution)/shard_map/all_to_all | solution.py:36
  16.8 3.1 copy-start.10
  19.2 3.9 collective-permute-start.1
  22.1 76.0 %collective-permute-start = (bf16[3584,256]{1,0:T(8,128)(2,1)}, bf16[3584,256]{1,0:T(8,128)(2,1)S(1)}, u32[]{:S(2)}, u32[]{:S(2)}) collective-permute-start(bf16[3584,256]{1,0:T(8,128)(2,1)} %get-tuple-element.40), channel_id=1, source_target_pairs={{0,1},{1,0},{2,3},{3,2},{4,5},{5,4},{6,7},{7,6},{8,9},{9,8},{10,11... | collective-permute-start | bytes 5505032 | tf_op jit(solution)/shard_map/ppermute | solution.py:32
  23.4 1.9 copy-start
  98.0 1.3 copy-start.3
  99.3 9.0 %copy-start.1 = (bf16[512,3584]{1,0:T(8,128)(2,1)S(1)}, bf16[512,3584]{1,0:T(8,128)(2,1)}, u32[]{:S(2)}) copy-start(bf16[512,3584]{1,0:T(8,128)(2,1)} %copy-done) | copy-start | bytes 11010052
  103.2 5.0 %collective-permute-start.2 = (f32[512,512]{1,0:T(8,128)S(1)}, f32[512,512]{1,0:T(8,128)S(1)}, u32[]{:S(2)}, u32[]{:S(2)}) collective-permute-start(f32[512,512]{1,0:T(8,128)S(1)} %shard_map.88.mine), channel_id=1, source_target_pairs={{0,1},{1,0},{2,3},{3,2},{4,5},{5,4},{6,7},{7,6},{8,9},{9,8},{10,11... | collective-permute-start | bytes 3145736 | tf_op jit(solution)/shard_map/ppermute | solution.py:32
  110.3 74.1 %copy-start.5 = (bf16[1,64,7168]{2,1,0:T(8,128)(2,1)S(1)}, bf16[1,64,7168]{2,1,0:T(8,128)(2,1)}, u32[]{:S(2)}) copy-start(bf16[1,64,7168]{2,1,0:T(8,128)(2,1)} %param.7) | copy-start | bytes 2752516
  110.4 74.1 %copy-start.6 = (bf16[1,64,7168]{2,1,0:T(8,128)(2,1)S(1)}, bf16[1,64,7168]{2,1,0:T(8,128)(2,1)}, u32[]{:S(2)}) copy-start(bf16[1,64,7168]{2,1,0:T(8,128)(2,1)} %param.8) | copy-start | bytes 2752516
  110.4 74.1 %copy-start.8 = (s32[1,2,2,64,1]{3,4,2,1,0:T(1,128)S(1)}, s32[1,2,2,64,1]{3,4,2,1,0:T(1,128)}, u32[]{:S(2)}) copy-start(s32[1,2,2,64,1]{3,4,2,1,0:T(1,128)} %param.10) | copy-start | bytes 3076
  110.4 74.1 %copy-start.9 = (f32[1,2,2,64,1]{3,4,2,1,0:T(1,128)S(1)}, f32[1,2,2,64,1]{3,4,2,1,0:T(1,128)}, u32[]{:S(2)}) copy-start(f32[1,2,2,64,1]{3,4,2,1,0:T(1,128)} %param.11) | copy-start | bytes 3076
  184.4 20.7 %copy-start.2 = (bf16[3584,256]{1,0:T(8,128)(2,1)S(1)}, bf16[3584,256]{1,0:T(8,128)(2,1)}, u32[]{:S(2)}) copy-start(bf16[3584,256]{1,0:T(8,128)(2,1)} %get-tuple-element.26.kept.refs_0_) | copy-start | bytes 5505028
  184.4 20.7 %copy-start.4 = (bf16[3584,256]{1,0:T(8,128)(2,1)S(1)}, bf16[3584,256]{1,0:T(8,128)(2,1)}, u32[]{:S(2)}) copy-start(bf16[3584,256]{1,0:T(8,128)(2,1)} %copy-done.3) | copy-start | bytes 5505028
  184.5 44.2 %copy-start.7 = (f32[1,7168]{1,0:T(1,128)S(1)}, f32[1,7168]{1,0:T(1,128)}, u32[]{:S(2)}) copy-start(f32[1,7168]{1,0:T(1,128)} %gain.3) | copy-start | bytes 86020
  185.9 38.8 %collective-permute-start.3 = (bf16[64,7168]{1,0:T(8,128)(2,1)S(1)}, bf16[64,7168]{1,0:T(8,128)(2,1)S(1)}, u32[]{:S(2)}, u32[]{:S(2)}) collective-permute-start(bf16[64,7168]{1,0:T(8,128)(2,1)S(1)} %get-tuple-element.24), channel_id=1, source_target_pairs={{0,32},{32,64},{64,96},{96,128},{128,160},{160,192},{192,224},{224... | collective-permute-start | bytes 2752520 | tf_op jit(solution)/shard_map/ppermute | solution.py:27
  205.1 23.6 %collective-permute-start.4 = (bf16[64,7168]{1,0:T(8,128)(2,1)S(1)}, bf16[64,7168]{1,0:T(8,128)(2,1)S(1)}, u32[]{:S(2)}, u32[]{:S(2)}) collective-permute-start(bf16[64,7168]{1,0:T(8,128)(2,1)S(1)} %get-tuple-element.25), channel_id=1, source_target_pairs={{0,224},{32,0},{64,32},{96,64},{128,96},{160,128},{192,160},{224,1... | collective-permute-start | bytes 2752520 | tf_op jit(solution)/shard_map/ppermute | solution.py:27
  322.4 3.5 collective-permute-start.5
